TPU v7x, 128 devices: a whole 4x4x4 slice. The times are simulated.
128 devices in a mesh: seq: 64 (over x, y, z), ch: 2 (over core).
Axes of the slice: x: 4, y: 4, z: 4, core: 2. Of those that a mesh axis runs over, the one named last changes fastest.
Arguments:
- resident_samples: bfloat16 [1024, 196608], P('ch', 'seq'), may hold values from -6 to 6
- worker_sample_counts: int32 [64], P('seq'), may hold values from 1024 to 3072, as said below
- spaced_tap_kernel: bfloat16 [5, 3, 512, 1024], P(None, None, 'ch'), may hold values from -0.109375 to 0.109375
- restore_kernel: bfloat16 [5, 1024, 512], P(None, None, 'ch'), may hold values from -0.25 to 0.25
- shrinking_kernel: bfloat16 [2, 4, 1024, 1024], P(None, None, 'ch'), may hold values from -0.09375 to 0.09375
- embedding_projector: bfloat16 [64, 1024], P(None, 'ch'), may hold values from -0.1875 to 0.1875
- quantizer_dictionary: float32 [64, 2048], replicated, may hold values from -5 to 5
Outputs:
- sharpest_tier_result: bfloat16 [1024, 131072], P('ch', 'seq')
- latent: float32 [64, 8192], P(None, 'seq')
- nearest: float32 [8192], P('seq')
Inputs may be any that keep to these rules, and one draw needn't show every extreme that they name: `worker_sample_counts`: the counts sum to 131072, and the sum of the counts of the loaders before loader d lies between d * 2048 and d * 2048 + 1024.
All inputs are finite; a program needn't handle non-finite values.
Results may differ from a plain program's by a relative error of at most 0.03.
Values may be sent and summed in bfloat16 or wider, within the bound.
A program may use at most 192 MiB of HBM per device.

v0:
```python
import jax
import jax.numpy as jnp
from jax import lax
from jax.sharding import PartitionSpec as P

EMB = 64
SHARD = 2048


dilation_rates = (1, 3, 1, 3, 3)


def padded_2(cells, sides, width):
    for axis, dim in sides:
        count = lax.axis_size(axis)
        ends = count - 1
        head = lax.slice_in_dim(cells, 0, width, axis=dim)
        tail = lax.slice_in_dim(cells, cells.shape[dim] - width, cells.shape[dim], axis=dim)
        cells = jnp.concatenate(
            [
                lax.ppermute(tail, axis, [(i, (i + 1) % count) for i in range(ends)]),
                cells,
                lax.ppermute(head, axis, [((i + 1) % count, i) for i in range(ends)]),
            ],
            axis=dim,
        )
    return cells


def entering(part, axis, combine, identity):
    place = lax.axis_index(axis)
    gathered = lax.all_gather(part, axis)
    state = jnp.zeros_like(part) + jnp.asarray(identity, part.dtype)

    def one(turn, state):
        return combine(state, lax.dynamic_index_in_dim(gathered, turn, 0, False))

    return lax.fori_loop(0, place, one, state)


def shifted(value, axis, steps):
    count = lax.axis_size(axis)
    leading, last = (max(0, -steps), min(count, count - steps))
    return lax.ppermute(value, axis, [(source, source + steps) for source in range(leading, last)])


def apply_residual(hidden_state, w_one, w_two, dilation):
    frames = hidden_state.shape[1]
    activated = jnp.maximum(hidden_state, jnp.zeros((), hidden_state.dtype))
    extended = padded_2(activated, (("seq", 1),), dilation)
    initial = jnp.zeros((w_one.shape[1], frames), jnp.float32)
    summed = initial
    pieces = lax.all_gather(extended, "ch", axis=0, tiled=True)
    for k in range(3):
        columns = w_one[k]
        summed = summed + jnp.dot(
            columns,
            pieces[:, k * dilation : k * dilation + frames],
            preferred_element_type=jnp.float32,
        )
    hidden = jnp.maximum(summed, 0.0).astype(jnp.bfloat16)
    update = lax.psum_scatter(
        jnp.dot(w_two, hidden, preferred_element_type=jnp.float32).astype(jnp.bfloat16),
        "ch",
        scatter_dimension=0,
        tiled=True,
    ).astype(jnp.float32)
    return (hidden_state.astype(jnp.float32) + update).astype(jnp.bfloat16)


def skipping_contraction(hidden_state, weight_params):
    initial = jnp.zeros((weight_params.shape[1], hidden_state.shape[1] // 4), jnp.float32)
    summed = initial
    pieces = lax.all_gather(hidden_state, "ch", axis=0, tiled=True)
    for k in range(4):
        columns = weight_params[k]
        summed = summed + jnp.dot(columns, pieces[:, k::4], preferred_element_type=jnp.float32)
    return summed.astype(jnp.bfloat16)


def on_device(
    resident_samples,
    worker_sample_counts,
    spaced_tap_kernel,
    restore_kernel,
    shrinking_kernel,
    embedding_projector,
    quantizer_dictionary,
):
    my_index = lax.axis_index("seq")
    before = entering(worker_sample_counts, "seq", lambda a, b: a + b, jnp.zeros((1,), jnp.int32))[
        0
    ]
    offset_in = (before - my_index * SHARD).astype(jnp.int32)
    spill_out = lax.dynamic_slice_in_dim(resident_samples, SHARD - offset_in, SHARD // 2, 1)
    spill_in = shifted(spill_out, "seq", 1)
    channels = resident_samples.shape[0]
    padded = jnp.concatenate(
        [jnp.zeros((channels, SHARD // 2), resident_samples.dtype), resident_samples], axis=1
    )
    own_frames = lax.dynamic_slice_in_dim(padded, SHARD // 2 - offset_in, SHARD, 1)
    spill_full = jnp.concatenate(
        [spill_in, jnp.zeros((channels, SHARD - SHARD // 2), resident_samples.dtype)], axis=1
    )
    column_ids = lax.broadcasted_iota(jnp.int32, (1, SHARD), 1)
    frame_stream = jnp.where(column_ids < offset_in, spill_full, own_frames)
    sharpest_tier_result = apply_residual(
        frame_stream, spaced_tap_kernel[0], restore_kernel[0], dilation_rates[0]
    )
    sharpest_tier_result = apply_residual(
        sharpest_tier_result, spaced_tap_kernel[1], restore_kernel[1], dilation_rates[1]
    )
    intermediate_tier = skipping_contraction(sharpest_tier_result, shrinking_kernel[0])
    intermediate_tier = apply_residual(
        intermediate_tier, spaced_tap_kernel[2], restore_kernel[2], dilation_rates[2]
    )
    intermediate_tier = apply_residual(
        intermediate_tier, spaced_tap_kernel[3], restore_kernel[3], dilation_rates[3]
    )
    lowest_resolution_tier = skipping_contraction(intermediate_tier, shrinking_kernel[1])
    lowest_resolution_tier = apply_residual(
        lowest_resolution_tier, spaced_tap_kernel[4], restore_kernel[4], dilation_rates[4]
    )
    partial_latent = jnp.dot(
        embedding_projector, lowest_resolution_tier, preferred_element_type=jnp.float32
    )
    latent = lax.psum(partial_latent.astype(jnp.bfloat16), "ch").astype(jnp.float32)
    latent_sq = jnp.sum(latent * latent, axis=0)
    code_sq = jnp.sum(quantizer_dictionary * quantizer_dictionary, axis=0)
    products = jnp.dot(latent.T, quantizer_dictionary, precision=lax.Precision.HIGHEST)
    distance = latent_sq[:, None] + code_sq[None, :] - 2.0 * products
    nearest = jnp.min(distance, axis=1) / EMB
    return (sharpest_tier_result, latent, nearest)


def solution(mesh):
    return jax.shard_map(
        on_device,
        mesh=mesh,
        in_specs=(
            P("ch", "seq"),
            P("seq"),
            P(None, None, "ch", None),
            P(None, None, "ch"),
            P(None, None, "ch", None),
            P(None, "ch"),
            P(),
        ),
        out_specs=(P("ch", "seq"), P(None, "seq"), P("seq")),
        check_vma=False,
    )
```

profile of v0, /device:TPU:1, one launch (start us, length us, event | category | flops | bytes accessed | tf_op | source)
XLA Modules:
  0.0 526.9 jit_solution(10902319453637519315)
XLA Ops:
  9.9 20.5 %all-reduce.2 = s32[64]{0:T(128)S(1)} all-reduce(s32[64]{0:T(128)S(1)} %dynamic-update-slice), channel_id=2, replica_groups=mesh['seq'=64,'ch'=2] {'seq'}, use_global_device_ids=true, to_apply=%add.2 | all-reduce | flops 64 | bytes 512
  30.3 3.2 copy.10
  34.8 4.8 collective-permute-start
  39.6 15.8 %collective-permute-done = bf16[512,1024]{0,1:T(8,128)(2,1)} collective-permute-done((bf16[512,1024]{0,1:T(8,128)(2,1)}, bf16[512,1024]{0,1:T(8,128)(2,1)}, u32[]{:S(2)}, u32[]{:S(2)}) %collective-permute-start) | collective-permute-done | bytes 1048608 | tf_op jit(solution)/shard_map/ppermute | solution.py:44
  55.4 2.6 broadcast_maximum_fusion.1
  59.4 4.1 collective-permute-start.1
  64.8 3.2 collective-permute-done.2
  68.0 12.9 %concatenate.23 = bf16[512,2050]{0,1:T(8,128)(2,1)} concatenate(bf16[512,1]{0,1:T(2,128)(2,1)S(1)} %collective-permute-done.1, bf16[512,2048]{0,1:T(8,128)(2,1)} %copy-done.3, bf16[512,1]{0,1:T(2,128)(2,1)S(1)} %collective-permute-done.2), dimensions={1} | concatenate | bytes 4198400 | tf_op jit(solution)/shard_map/concatenate | solution.py:19
  80.9 94.2 %all-gather.8.cloned.1.call-done = bf16[1024,2050]{0,1:T(8,128)(2,1)} async-done(((bf16[512,2050]{0,1:T(8,128)(2,1)}), bf16[1024,2050]{0,1:T(8,128)(2,1)}) %all-gather.8.cloned.1.call-update) | async-done | bytes 4198416 | tf_op jit(solution)/shard_map/all_gather | solution.py:53
  175.1 5.1 fusion.6
  180.2 3.8 fusion.8
  184.0 9.8 %convert_bitcast_fusion.1 = bf16[1024,2048]{0,1:T(8,128)(2,1)} fusion(f32[2048,256]{1,0:T(8,128)} %fusion.6, f32[2048,256]{1,0:T(8,128)} %fusion.8, bf16[1024,2050]{0,1:T(8,128)(2,1)} %all-gather.8.cloned.1.call-done, bf16[5,1024,256]{2,1,0:T(8,128)(2,1)} %param.12, bf16[5,3,256,1024]{3,2,1,0:T(8,128)(2,1)} %param.11), kind=kOutput, calls=%fused_computation.16 | convolution fusion | flops 2151677952 | bytes 13631488 | tf_op jit(solution)/shard_map/dot_general | solution.py:63
  193.9 16.1 %reduce-scatter.6.cloned.1.call-done = bf16[512,2048]{0,1:T(8,128)(2,1)} async-done(((bf16[1024,2048]{0,1:T(8,128)(2,1)}), bf16[512,2048]{0,1:T(8,128)(2,1)}) %reduce-scatter.6.cloned.1.call-update) | async-done | bytes 2097168 | tf_op jit(solution)/shard_map/reduce_scatter | solution.py:62
  210.0 3.2 broadcast_maximum_fusion
  214.5 3.3 collective-permute-start.3
  219.2 3.0 collective-permute-done.4
  222.2 12.9 %concatenate.24 = bf16[512,2054]{0,1:T(8,128)(2,1)} concatenate(bf16[512,3]{0,1:T(4,128)(2,1)S(1)} %collective-permute-done.3, bf16[512,2048]{0,1:T(8,128)(2,1)} %copy-done.2, bf16[512,3]{0,1:T(4,128)(2,1)S(1)} %collective-permute-done.4), dimensions={1} | concatenate | bytes 4206592 | tf_op jit(solution)/shard_map/concatenate | solution.py:19
  235.4 22.1 %all-gather.10.cloned.1.call-done = bf16[1024,2054]{0,1:T(8,128)(2,1)} async-done(((bf16[512,2054]{0,1:T(8,128)(2,1)}), bf16[1024,2054]{0,1:T(8,128)(2,1)}) %all-gather.10.cloned.1.call-update) | async-done | bytes 4206608 | tf_op jit(solution)/shard_map/all_gather | solution.py:53
  257.5 5.1 fusion
  262.6 3.8 fusion.2
  266.4 9.9 %convert_bitcast_fusion = bf16[1024,2048]{0,1:T(8,128)(2,1)} fusion(f32[2048,256]{1,0:T(8,128)} %fusion, f32[2048,256]{1,0:T(8,128)} %fusion.2, bf16[1024,2054]{0,1:T(8,128)(2,1)} %all-gather.10.cloned.1.call-done, bf16[5,1024,256]{2,1,0:T(8,128)(2,1)} %param.12, bf16[5,3,256,1024]{3,2,1,0:T(8,128)(2,1)} %param.11), kind=kOutput, calls=%fused_computation.14 | convolution fusion | flops 2151677952 | bytes 13631488 | tf_op jit(solution)/shard_map/dot_general | solution.py:63
  276.3 16.1 %reduce-scatter.8.cloned.1.call-done = bf16[512,2048]{0,1:T(8,128)(2,1)} async-done(((bf16[1024,2048]{0,1:T(8,128)(2,1)}), bf16[512,2048]{0,1:T(8,128)(2,1)}) %reduce-scatter.8.cloned.1.call-update) | async-done | bytes 2097168 | tf_op jit(solution)/shard_map/reduce_scatter | solution.py:62
  292.5 4.6 add_convert_fusion
  297.2 18.0 %all-gather.12.cloned.1.call-done = bf16[1024,2048]{0,1:T(8,128)(2,1)} async-done(((bf16[512,2048]{0,1:T(8,128)(2,1)}), bf16[1024,2048]{0,1:T(8,128)(2,1)}) %all-gather.12.cloned.1.call-update) | async-done | bytes 4194320 | tf_op jit(solution)/shard_map/all_gather | solution.py:74
  315.2 8.6 %slice.254 = bf16[1024,512]{0,1:T(8,128)(2,1)S(1)} slice(bf16[1024,2048]{0,1:T(8,128)(2,1)} %all-gather.12.cloned.1.call-done), slice={[0:1024:1], [0:2048:4]} | slice | bytes 2097152 | tf_op jit(solution)/shard_map/slice | solution.py:77
  325.8 8.6 %slice.256 = bf16[1024,512]{0,1:T(8,128)(2,1)S(1)} slice(bf16[1024,2048]{0,1:T(8,128)(2,1)} %all-gather.12.cloned.1.call-done), slice={[0:1024:1], [1:2048:4]} | slice | bytes 2097152 | tf_op jit(solution)/shard_map/slice | solution.py:77
  336.4 8.6 %slice.258 = bf16[1024,512]{0,1:T(8,128)(2,1)S(1)} slice(bf16[1024,2048]{0,1:T(8,128)(2,1)} %all-gather.12.cloned.1.call-done), slice={[0:1024:1], [2:2048:4]} | slice | bytes 2097152 | tf_op jit(solution)/shard_map/slice | solution.py:77
  347.1 8.6 %slice.260 = bf16[1024,512]{0,1:T(8,128)(2,1)S(1)} slice(bf16[1024,2048]{0,1:T(8,128)(2,1)} %all-gather.12.cloned.1.call-done), slice={[0:1024:1], [3:2048:4]} | slice | bytes 2097152 | tf_op jit(solution)/shard_map/slice | solution.py:77
  358.1 3.3 collective-permute-start.5
  364.0 3.8 collective-permute-done.6
  369.3 17.4 %all-gather.14.cloned.1.call-done = bf16[1024,514]{1,0:T(8,128)(2,1)} async-done(((bf16[512,514]{1,0:T(8,128)(2,1)}), bf16[1024,514]{1,0:T(8,128)(2,1)}) %all-gather.14.cloned.1.call-update) | async-done | bytes 1052688 | tf_op jit(solution)/shard_map/all_gather | solution.py:53
  386.7 2.4 fusion.62
  391.0 3.8 fusion.38
  394.9 12.7 %reduce-scatter.10.cloned.1.call-done = bf16[512,512]{0,1:T(8,128)(2,1)} async-done(((bf16[1024,512]{0,1:T(8,128)(2,1)}), bf16[512,512]{0,1:T(8,128)(2,1)}) %reduce-scatter.10.cloned.1.call-update) | async-done | bytes 524304 | tf_op jit(solution)/shard_map/reduce_scatter | solution.py:62
  408.7 3.3 collective-permute-start.7
  413.3 3.0 collective-permute-done.8
  417.4 17.6 %all-gather.16.cloned.1.call-done = bf16[1024,518]{0,1:T(8,128)(2,1)} async-done(((bf16[512,518]{0,1:T(8,128)(2,1)}), bf16[1024,518]{0,1:T(8,128)(2,1)}) %all-gather.16.cloned.1.call-update) | async-done | bytes 1060880 | tf_op jit(solution)/shard_map/all_gather | solution.py:53
  438.7 3.5 fusion.39
  442.3 12.7 %reduce-scatter.12.cloned.1.call-done = bf16[512,512]{0,1:T(8,128)(2,1)} async-done(((bf16[1024,512]{0,1:T(8,128)(2,1)}), bf16[512,512]{0,1:T(8,128)(2,1)}) %reduce-scatter.12.cloned.1.call-update) | async-done | bytes 524304 | tf_op jit(solution)/shard_map/reduce_scatter | solution.py:62
  457.1 13.2 %all-gather.18.cloned.1.call-done = bf16[1024,512]{0,1:T(8,128)(2,1)} async-done(((bf16[512,512]{0,1:T(8,128)(2,1)}), bf16[1024,512]{0,1:T(8,128)(2,1)}) %all-gather.18.cloned.1.call-update) | async-done | bytes 1048592 | tf_op jit(solution)/shard_map/all_gather | solution.py:74
  470.3 2.3 slice.280
  474.3 2.2 slice.282
  484.3 4.0 collective-permute-start.9
  489.1 3.0 all_gather.35
  494.8 2.7 fusion.50
  497.6 2.4 copy.13
  499.9 14.1 %reduce-scatter.14.cloned.1.call-done = bf16[512,128]{0,1:T(8,128)(2,1)} async-done(((bf16[1024,128]{0,1:T(8,128)(2,1)}), bf16[512,128]{0,1:T(8,128)(2,1)}) %reduce-scatter.14.cloned.1.call-update) | async-done | bytes 131088 | tf_op jit(solution)/shard_map/reduce_scatter | solution.py:62
  515.1 3.4 psum.7
  (94 shorter events, 48.5 us)
Async XLA Ops:
  7.2 506.9 %copy-start = (bf16[64,512]{1,0:T(8,128)(2,1)S(1)}, bf16[64,512]{1,0:T(8,128)(2,1)}, u32[]{:S(2)}) copy-start(bf16[64,512]{1,0:T(8,128)(2,1)} %param.14) | copy-start | bytes 196612
  7.2 167.9 %all-gather.8.cloned.1.call-start = ((), (), s32[]{:S(2)}) async-start(), calls=%async_computation.5 | async-start | bytes 6316032 | tf_op jit(solution)/shard_map/all_gather | solution.py:53
  34.8 20.7 %collective-permute-start = (bf16[512,1024]{0,1:T(8,128)(2,1)}, bf16[512,1024]{0,1:T(8,128)(2,1)}, u32[]{:S(2)}, u32[]{:S(2)}) collective-permute-start(bf16[512,1024]{0,1:T(8,128)(2,1)} %constant_dynamic-slice_fusion.1), channel_id=1, source_target_pairs={{0,2},{2,4},{4,6},{6,8},{8,10},{10,12},{12,14},{14,16},{16,18},{18... | collective-permute-start | bytes 3145736 | tf_op jit(solution)/shard_map/ppermute | solution.py:44
  58.1 1.3 copy-start.3
  59.4 5.4 %collective-permute-start.1 = (bf16[512,1]{0,1:T(2,128)(2,1)S(1)}, bf16[512,1]{0,1:T(2,128)(2,1)S(1)}, u32[]{:S(2)}, u32[]{:S(2)}) collective-permute-start(bf16[512,1]{0,1:T(2,128)(2,1)S(1)} %get-tuple-element.43), channel_id=1, source_target_pairs={{0,2},{2,4},{4,6},{6,8},{8,10},{10,12},{12,14},{14,16},{16,18},{18... | collective-permute-start | bytes 3080 | tf_op jit(solution)/shard_map/ppermute | solution.py:21
  63.5 4.5 collective-permute-start.2
  80.8 129.1 %reduce-scatter.6.cloned.1.call-start = ((), (), s32[]{:S(2)}) async-start(), calls=%async_computation.6 | async-start | bytes 6291456 | tf_op jit(solution)/shard_map/reduce_scatter | solution.py:62
  175.1 5.1 copy-start.7
  193.8 63.7 %all-gather.10.cloned.1.call-start = ((), (), s32[]{:S(2)}) async-start(), calls=%async_computation.7 | async-start | bytes 6316032 | tf_op jit(solution)/shard_map/all_gather | solution.py:53
  213.2 1.3 copy-start.2
  214.5 4.7 collective-permute-start.3
  217.9 4.4 collective-permute-start.4
  235.1 57.4 %reduce-scatter.8.cloned.1.call-start = ((), (), s32[]{:S(2)}) async-start(), calls=%async_computation.8 | async-start | bytes 6291456 | tf_op jit(solution)/shard_map/reduce_scatter | solution.py:62
  257.5 5.1 copy-start.8
  276.3 38.9 %all-gather.12.cloned.1.call-start = ((), (), s32[]{:S(2)}) async-start(), calls=%async_computation.9 | async-start | bytes 6291456 | tf_op jit(solution)/shard_map/all_gather | solution.py:74
  297.1 89.6 %all-gather.14.cloned.1.call-start = ((), (), s32[]{:S(2)}) async-start(), calls=%async_computation.10 | async-start | bytes 1966080 | tf_op jit(solution)/shard_map/all_gather | solution.py:53
  358.1 6.0 %collective-permute-start.5 = (bf16[512,1]{1,0:T(8,128)(2,1)S(1)}, bf16[512,1]{1,0:T(8,128)(2,1)S(1)}, u32[]{:S(2)}, u32[]{:S(2)}) collective-permute-start(bf16[512,1]{1,0:T(8,128)(2,1)S(1)} %get-tuple-element.46), channel_id=1, source_target_pairs={{0,2},{2,4},{4,6},{6,8},{8,10},{10,12},{12,14},{14,16},{16,18},{18... | collective-permute-start | bytes 3080 | tf_op jit(solution)/shard_map/ppermute | solution.py:21
  361.4 6.5 %collective-permute-start.6 = (bf16[512,1]{1,0:T(8,128)(2,1)S(1)}, bf16[512,1]{1,0:T(8,128)(2,1)S(1)}, u32[]{:S(2)}, u32[]{:S(2)}) collective-permute-start(bf16[512,1]{1,0:T(8,128)(2,1)S(1)} %get-tuple-element.47), channel_id=1, source_target_pairs={{2,0},{4,2},{6,4},{8,6},{10,8},{12,10},{14,12},{16,14},{18,16},{20... | collective-permute-start | bytes 3080 | tf_op jit(solution)/shard_map/ppermute | solution.py:23
  369.1 38.4 %reduce-scatter.10.cloned.1.call-start = ((), (), s32[]{:S(2)}) async-start(), calls=%async_computation.11 | async-start | bytes 1572864 | tf_op jit(solution)/shard_map/reduce_scatter | solution.py:62
  386.7 4.2 copy-start.9
  394.8 40.1 %all-gather.16.cloned.1.call-start = ((), (), s32[]{:S(2)}) async-start(), calls=%async_computation.12 | async-start | bytes 1597440 | tf_op jit(solution)/shard_map/all_gather | solution.py:53
  408.7 4.6 collective-permute-start.7
  412.0 4.4 collective-permute-start.8
  417.3 37.7 %reduce-scatter.12.cloned.1.call-start = ((), (), s32[]{:S(2)}) async-start(), calls=%async_computation.13 | async-start | bytes 1572864 | tf_op jit(solution)/shard_map/reduce_scatter | solution.py:62
  434.9 3.8 copy-start.10
  438.7 16.3 %copy-start.4 = (bf16[512,512]{0,1:T(8,128)(2,1)S(1)}, bf16[512,512]{0,1:T(8,128)(2,1)}, u32[]{:S(2)}) copy-start(bf16[512,512]{0,1:T(8,128)(2,1)} %reduce-scatter.10.cloned.1.call-done) | copy-start | bytes 1572868
  442.3 28.0 %all-gather.18.cloned.1.call-start = ((), (), s32[]{:S(2)}) async-start(), calls=%async_computation.14 | async-start | bytes 1572864 | tf_op jit(solution)/shard_map/all_gather | solution.py:74
  457.1 57.0 %reduce-scatter.14.cloned.1.call-start = ((), (), s32[]{:S(2)}) async-start(), calls=%async_computation.15 | async-start | bytes 393216 | tf_op jit(solution)/shard_map/reduce_scatter | solution.py:62
  470.3 8.0 %copy-start.5 = (bf16[1024,512]{0,1:T(8,128)(2,1)S(1)}, bf16[1024,512]{0,1:T(8,128)(2,1)}, u32[]{:S(2)}) copy-start(bf16[1024,512]{0,1:T(8,128)(2,1)} %all-gather.18.cloned.1.call-done) | copy-start | bytes 3145732
  480.6 16.9 %copy-start.6 = (f32[64,2048]{1,0:T(8,128)S(1)}, f32[64,2048]{1,0:T(8,128)}, u32[]{:S(2)}) copy-start(f32[64,2048]{1,0:T(8,128)} %param.15) | copy-start | bytes 1572868
  481.1 16.5 %copy-start.1 = (bf16[512,2048]{0,1:T(8,128)(2,1)S(1)}, bf16[512,2048]{0,1:T(8,128)(2,1)}, u32[]{:S(2)}) copy-start(bf16[512,2048]{0,1:T(8,128)(2,1)} %add_convert_fusion) | copy-start | bytes 6291460
  483.0 5.3 %collective-permute-start.10 = (bf16[512,3]{0,1:T(4,128)(2,1)S(1)}, bf16[512,3]{0,1:T(4,128)(2,1)S(1)}, u32[]{:S(2)}, u32[]{:S(2)}) collective-permute-start(bf16[512,3]{0,1:T(4,128)(2,1)S(1)} %get-tuple-element.49), channel_id=1, source_target_pairs={{2,0},{4,2},{6,4},{8,6},{10,8},{12,10},{14,12},{16,14},{18,16},{20... | collective-permute-start | bytes 9224 | tf_op jit(solution)/shard_map/ppermute | solution.py:23
  484.3 4.7 collective-permute-start.9
Sparse Core Ops, SparseCore 0:
  81.0 94.0 all-gather.7
  193.9 16.0 reduce-scatter.5
  235.2 22.1 all-gather.9
  276.4 16.0 reduce-scatter.7
  297.3 17.8 all-gather.11
  369.2 17.4 all-gather.13
  394.9 12.5 reduce-scatter.9
  417.5 17.4 all-gather.15
  442.4 12.5 reduce-scatter.11
  457.2 13.0 all-gather.17
  497.6 16.4 reduce-scatter.13
where the time goes:
time: 530 us; the launch traced here: 527 us
  waiting for transfers between devices  285 us (54%)
  local copies, waits for them, and re-layouts  77.7 us (15%)
  matrix products  74.7 us (14%)
  starting transfers between devices  30.1 us (6%)
  blocking collectives  26.8 us (5%)
  other arithmetic  17.2 us (3%)
  between operations  15 us (3%)
    all_gather x4, waiting for transfers between devices, apply_residual(): pieces = lax.all_gather(extended, 'ch', axis=0, tiled=True)  151 us
    reduce_scatter x5, waiting for transfers between devices, apply_residual(): lax.psum_scatter(jnp.dot(w_two, hidden, preferred_element_type=jnp.float3...  71.7 us
    slice x8, local copies, waits for them, and re-layouts, skipping_contraction(): pieces[:, k::4]  40.2 us
    all_gather x2, waiting for transfers between devices, skipping_contraction(): pieces = lax.all_gather(hidden_state, 'ch', axis=0, tiled=True)  31.2 us
    dot_general x5, matrix products, apply_residual(): jnp.dot(w_two, hidden, preferred_element_type=jnp.float32)  29.6 us
    dot_general x10, matrix products, apply_residual(): jnp.dot(columns, pieces[:, k * dilation:k * dilation + frames], preferred...  28.5 us
    concatenate x2, local copies, waits for them, and re-layouts, padded_2(): jnp.concatenate([lax.ppermute(tail, axis, [(i, (i + 1) % count) for i in...  25.7 us
    unnamed x1, blocking collectives  20.5 us
  transfers between devices with their start and end apart: 22, of which 18 were waited for; matrix products, arithmetic and copies ran while one was open for 0% of the time, Pallas kernels for 0%

commit v1 on v0

v1 whole, which is shorter than its diff:
```python
import jax
import jax.numpy as jnp
from jax import lax
from jax.experimental import pallas as pl
from jax.experimental.pallas import tpu as pltpu
from jax.sharding import PartitionSpec as P

MESH = pl.DeviceIdType.MESH
BF, F32, I32 = jnp.bfloat16, jnp.float32, jnp.int32
C, H, EMB, BINS, SHARD, CAP = 1024, 512, 64, 2048, 2048, 3072
T = 304
T2 = 80
HEAD = 24
PAD = 32
EDGE = 2 * T


def nt(a, b):
    return lax.dot_general(a, b, (((1,), (1,)), ((), ())), preferred_element_type=F32)


def nn(a, b):
    return jnp.dot(a, b, preferred_element_type=F32)


def iota(shape, dim):
    return lax.broadcasted_iota(I32, shape, dim)


def ones_where(mask):
    return jnp.where(mask, 1.0, 0.0).astype(BF)


def kernel(
    cnt_ref, res_hbm, w1_hbm, w2_hbm, dn_hbm, pj_hbm, cb_hbm,
    out_hbm, lat_ref, near_ref,
    res, w1, w2, dn, pj, cb, cbk, counts, place, edge, send_r, send_rr, shift, x, a, pb, carry, hid, y32, z, u, v, ot,
    msg, msg_peer, msg_left,
    lsem, rsem, wsend, wrecv, csend, crecv, esend, erecv, hsend, hrecv, olocal, osend, opeer, oleft, msend, mrecv,
):
    s, c = lax.axis_index("seq"), lax.axis_index("ch")
    n_seq = lax.axis_size("seq")
    right, left = lax.rem(s + 1, n_seq), lax.rem(s + n_seq - 1, n_seq)
    other = 1 - c
    peer = {"seq": s, "ch": other}
    rounds = ((lax.rem(s, 4), 1), (lax.rem(s // 4, 4), 4), (s // 16, 16))
    last = (s == n_seq - 1) & (c == 1)

    def remote(src, dst, send, recv, where):
        return pltpu.make_async_remote_copy(
            src_ref=src, dst_ref=dst, send_sem=send, recv_sem=recv, device_id=where, device_id_type=MESH
        )

    def weight(i, on):
        if i < 15:
            b, k = divmod(i, 3)
            tap = k + (1 - on) * (2 - 2 * k)
            return w1_hbm.at[b, k], w1.at[b, pl.ds(pl.multiple_of(512 * tap + 256 * c, 256), 256)]
        if i < 20:
            return w2_hbm.at[i - 15], w2.at[i - 15, :, pl.ds(pl.multiple_of(256 * c, 256), 256)]
        if i < 28:
            l, k = divmod(i - 20, 4)
            tap = k + (1 - on) * (3 - 2 * k)
            return dn_hbm.at[l, k], dn.at[
                l, pl.ds(pl.multiple_of(512 * c, 512), 512), pl.ds(pl.multiple_of(1024 * tap, 1024), 1024)
            ]
        return pj_hbm, pj.at[pl.ds(0, EMB), pl.ds(pl.multiple_of(512 * c, 512), 512)]

    def weight_local(i):
        return pltpu.make_async_copy(*weight(i, c), lsem.at[i])

    def weight_remote(i):
        return remote(*weight(i, other), wsend.at[i], wrecv.at[i], peer)

    def block_weights(b):
        return [3 * b, 3 * b + 1, 3 * b + 2, 15 + b]

    def down_weights(l):
        return [20 + 4 * l + k for k in range(4)]

    def need(items):
        for i in items:
            weight_local(i).wait()
            weight_remote(i).wait_recv()

    groups = [
        block_weights(0) + block_weights(1),
        down_weights(0) + block_weights(2),
        block_weights(3) + down_weights(1) + block_weights(4) + [28],
    ]
    load_res = [
        pltpu.make_async_copy(res_hbm.at[:, pl.ds(128 * k, 128)], res.at[k], rsem.at[k]) for k in range(CAP // 128)
    ]
    load_cb = pltpu.make_async_copy(cb_hbm, cb, lsem.at[30])
    for copy in load_res:
        copy.start()
    load_cb.start()

    barrier = pltpu.get_barrier_semaphore()
    greeted = [peer] + [{"seq": chip, "ch": core} for chip in (left, right) for core in (0, 1)]
    partners = [[], [], []]
    for dim, (at, stride) in enumerate(rounds):
        for q in (1, 2, 3):
            j = lax.rem(at + q, 4)
            partners[dim].append((j, {"seq": s + (j - at) * stride, "ch": c}))
            greeted.append(partners[dim][-1][1])
    for where in greeted:
        pl.semaphore_signal(barrier, inc=1, device_id=where, device_id_type=MESH)

    cnt = cnt_ref[0]
    x[0:PAD, :] = jnp.zeros((PAD, C), BF)
    pb[...] = jnp.zeros(pb.shape, F32)
    carry[...] = jnp.zeros(carry.shape, F32)

    def picked(first, sign):
        lowest = jnp.maximum(jnp.minimum(first, first + sign * (T - 1)), 0)
        tile = jnp.minimum(lax.shift_right_logical(lowest, 7), CAP // 128 - 4)
        column = 128 * tile + iota((T, 512), 1)
        pick = ones_where((column == first + sign * iota((T, 512), 0)) & (column < cnt))
        found = jnp.concatenate([res[tile + q] for q in range(4)], axis=1)
        return nt(pick, found).astype(BF)

    def count_round(dim, value):
        at = rounds[dim][0]
        counts[dim, at] = value
        copies = []
        for q, (j, where) in enumerate(partners[dim]):
            copies.append(
                remote(counts.at[dim, at], counts.at[dim, at], csend.at[dim, q], crecv.at[dim, at], where)
            )
            copies[-1].start()
        return copies

    def count_sums(dim):
        at = rounds[dim][0]
        for q, (j, where) in enumerate(partners[dim]):
            remote(counts.at[dim, j], counts.at[dim, j], csend.at[dim, q], crecv.at[dim, j], where).wait_recv()
        before, total = jnp.zeros((8, 128), I32), jnp.zeros((8, 128), I32)
        for j in range(4):
            value = counts[dim, j]
            total = total + value
            before = before + jnp.where(j < at, value, 0)
        return before, total

    half_c = pl.ds(pl.multiple_of(512 * c, 512), 512)
    sends = []

    def send_edges(m):
        for q, (buffer, where) in enumerate(
            ((send_r, {"seq": right, "ch": 0}), (send_rr, {"seq": left, "ch": 1}))
        ):
            copy = remote(buffer.at[m], edge.at[m, :, half_c], esend.at[m, q], erecv.at[m, c], where)
            copy.start()
            sends.append(copy)

    for copy in load_res:
        copy.wait()
    for i in groups[0]:
        weight_local(i).start()
    pl.semaphore_wait(barrier, len(greeted))
    sends += count_round(0, jnp.full((8, 128), cnt, I32))
    send_r[0] = picked(cnt - 1, -1)
    send_rr[0] = picked(jnp.int32(0), 1)
    send_edges(0)
    before, total = count_sums(0)
    sends += count_round(1, total)
    for i in groups[0]:
        sends.append(weight_remote(i))
        sends[-1].start()
    send_r[1] = picked(cnt - 1 - T, -1)
    send_rr[1] = picked(jnp.int32(T), 1)
    send_edges(1)
    more, total = count_sums(1)
    before = before + more
    sends += count_round(2, total)
    for g in (1, 2):
        for i in groups[g]:
            weight_local(i).start()
    more, total = count_sums(2)
    place[...] = before + more - SHARD * s
    offset = place[0, 0]
    gap = jnp.where(c == 0, SHARD // 2 - offset, offset + cnt - SHARD)

    def window(core, n):
        sign = 2 * core - 1
        first = jnp.where(core == 1, 1440, 1631) + sign * T * n - offset
        return picked(first, sign)

    def to_peer(h):
        rows = pl.ds(PAD + EDGE * h, EDGE)
        return remote(shift.at[h], x.at[rows, half_c], hsend.at[h], hrecv.at[h], peer)

    for h in (0, 1):

        def shifted(n, _):
            shift[h, pl.ds(pl.multiple_of(T * n, 16), T), :] = window(other, 2 * h + n)
            return 0

        lax.fori_loop(0, 2, shifted, 0)
        sends.append(to_peer(h))
        sends[-1].start()

    def placed(n, _):
        x[pl.ds(pl.multiple_of(PAD + T * n, 16), T), half_c] = window(c, n)
        return 0

    lax.fori_loop(0, 4, placed, 0)
    for i in groups[1]:
        sends.append(weight_remote(i))
        sends[-1].start()

    def block(ref, at, rows, b, dilation, lag, bound, wide_at):
        def tap(n, _):
            lanes = pl.ds(pl.multiple_of(256 * n, 256), 256)
            pb[HEAD : HEAD + rows, lanes] = nt(a[:rows, :], w1[b, lanes, :])
            return 0

        lax.fori_loop(0, 6, tap, 0)

        def hide(n, _):
            here = HEAD - lag

            def product(k, start):
                return pb[start : start + rows, pl.ds(pl.multiple_of(512 * k + 128 * n, 128), 128)]

            p0, p1, p2 = product(0, here - dilation), product(1, here), product(2, here + dilation)
            if bound is not None:
                t = iota((rows, 128), 0) - jnp.where(last, bound, 1 << 20)
                p0 = jnp.where((t >= 0) & (t < dilation), 0.0, p0)
                p2 = jnp.where((t < 0) & (t >= -dilation), 0.0, p2)
            hid[:rows, pl.ds(pl.multiple_of(128 * n, 128), 128)] = jnp.maximum(p0 + p1 + p2, 0.0).astype(BF)
            return 0

        lax.fori_loop(0, 4, hide, 0)
        if lag:
            carry[b] = pb[rows : rows + HEAD, :]

        def back(n, _):
            lanes = pl.ds(pl.multiple_of(256 * n, 256), 256)
            update = nt(hid[:rows, :], w2[b, lanes, :])
            new = (ref[at : at + rows, lanes].astype(F32) + update).astype(BF)
            ref[at : at + rows, lanes] = new
            if wide_at is not None:
                for q in (0, 1):
                    y32[2 * n + q, wide_at : wide_at + rows, :] = new[:, 128 * q : 128 * (q + 1)].astype(F32)
            return 0

        lax.fori_loop(0, 4, back, 0)

    def out_tile(i):
        r, q = iota((256, 256), 0), iota((256, 256), 1)
        order = ones_where(jnp.where(c == 0, 255 - r, r) == q)
        same = ones_where(r == q)

        def turn(n, _):
            lanes = pl.ds(pl.multiple_of(256 * n, 256), 256)
            rows = nn(order, x[PAD + 96 + 256 * i : PAD + 352 + 256 * i, lanes]).astype(BF)
            ot[i, lanes, :] = nt(same, rows).astype(BF)
            return 0

        lax.fori_loop(0, 4, turn, 0)

    def half(core):
        return pl.ds(pl.multiple_of(512 * core, 512), 512)

    def own_tile(i, start):
        columns = pl.ds(pl.multiple_of(start, 256), 256)
        return (
            pltpu.make_async_copy(ot.at[i, half(c)], out_hbm.at[:, columns], olocal.at[i]),
            remote(ot.at[i, half(other)], out_hbm.at[:, columns], osend.at[i, 0], opeer.at[i], peer),
        )

    def next_tile(i):
        columns = pl.ds(256 * (i - 2), 256)
        return [
            remote(
                ot.at[i, pl.ds(512 * core, 512)],
                out_hbm.at[:, columns],
                osend.at[i, core],
                oleft.at[i - 2],
                {"seq": right, "ch": core},
            )
            for core in (0, 1)
        ]

    def emit(i):
        out_tile(i)
        if i < 2:
            for copy in own_tile(i, jnp.where(c == 0, 1280 - 256 * i, 1536 + 256 * i)):
                copy.start()
        else:

            @pl.when(c == 0)
            def _():
                for copy in own_tile(i, 1280 - 256 * i):
                    copy.start()

            @pl.when(c == 1)
            def _():
                for copy in next_tile(i):
                    copy.start()

    for n in range(4):
        at = PAD + T * n
        if n % 2 == 0:
            to_peer(n // 2).wait_recv()
        if n >= 2:
            m = n - 2
            for core in (0, 1):
                remote(
                    send_r.at[m], edge.at[m, :, pl.ds(512 * core, 512)], esend.at[m, 0], erecv.at[m, core],
                    {"seq": right, "ch": 0},
                ).wait_recv()
            picks = [
                ones_where(T * e + iota((T, T), 1) == T * m + iota((T, T), 0) - gap) for e in range(m + 1)
            ]

            def fill(q, _):
                lanes = pl.ds(pl.multiple_of(256 * q, 256), 256)
                total = x[at : at + T, lanes].astype(F32)
                for e in range(m + 1):
                    total = total + nn(picks[e], edge[e, :, lanes])
                x[at : at + T, lanes] = total.astype(BF)
                return 0

            lax.fori_loop(0, 4, fill, 0)
        for b, dilation in ((0, 1), (1, 3)):
            if n == 0:
                need(block_weights(b))
            start = at - 16 * b
            a[...] = jnp.maximum(x[start : start + T, :], jnp.zeros((), BF))
            pb[0:HEAD, :] = carry[b]
            bound = EDGE - (T * n - 16 * b - 16) if n == 2 else None
            block(x, start - 16, T, b, dilation, 16, bound, T * n if b == 1 else None)
        if n == 0:
            for i in groups[2]:
                sends.append(weight_remote(i))
                sends[-1].start()
        for i in ((), (0,), (1, 2), (3,))[n]:
            emit(i)

    def fold(rows):
        def one(n, _):
            for k in range(4):
                lanes = pl.ds(pl.multiple_of(1024 * k + 128 * n, 128), 128)
                z[:rows, lanes] = y32[n, pl.ds(k, rows, stride=4), :].astype(BF)
            return 0

        lax.fori_loop(0, 8, one, 0)

    fold(T)
    need(down_weights(0))

    def down(l, rows, to):
        def one(n, _):
            lanes = pl.ds(pl.multiple_of(256 * n, 256), 256)
            to[:, lanes] = nt(z[:rows, :], dn[l, lanes, :]).astype(BF)
            return 0

        lax.fori_loop(0, 4, one, 0)

    down(0, T, u)
    for b, dilation in ((2, 1), (3, 3)):
        need(block_weights(b))
        a[...] = jnp.maximum(u[...], jnp.zeros((), BF))
        block(u, 0, T, b, dilation, 0, 160, 0 if b == 3 else None)

    fold(T2)
    need(down_weights(1))
    down(1, T2, v)
    need(block_weights(4))
    a[:T2, :] = jnp.maximum(v[...], jnp.zeros((), BF))
    block(v, 0, T2, 4, 3, 0, 40, None)

    need([28])
    load_cb.wait()
    pj[EMB : 2 * EMB, :] = pj[0:EMB, :]
    pj[2 * EMB : 3 * EMB, :] = pj[0:EMB, :]
    book = cb[...]
    book_hi = book.astype(BF)
    cbk[0:EMB, :] = book_hi
    cbk[EMB : 2 * EMB, :] = book_hi
    cbk[2 * EMB : 3 * EMB, :] = (book - book_hi.astype(F32)).astype(BF)
    book_sq = jnp.sum(book * book, axis=0, keepdims=True)
    frame, row = iota((128, T2), 0), iota((128, T2), 1)
    spot = jnp.where(c == 0, 103 - row, lax.rem(88 + row, 128))
    coarse = nn(ones_where((spot == frame) & (row >= 8) & (row < 72)), v[...]).astype(BF)
    latent = nt(pj[0:EMB, :], coarse)
    thrice = nt(coarse, pj[...])
    hi = thrice.astype(BF)
    lo = (thrice - hi.astype(F32)).astype(BF)
    lane = iota((128, 3 * EMB), 1)
    lhs = jnp.where((lane >= EMB) & (lane < 2 * EMB), lo, hi)
    nearest = jnp.full((128, 1), jnp.inf, F32)
    for q in range(4):
        columns = slice(512 * q, 512 * (q + 1))
        distance = book_sq[:, columns] - 2.0 * nn(lhs, cbk[:, columns])
        nearest = jnp.minimum(nearest, jnp.min(distance, axis=1, keepdims=True))
    diagonal = iota((128, 128), 0) == iota((128, 128), 1)
    nearest = jnp.sum(jnp.where(diagonal, nearest, 0.0), axis=0, keepdims=True)
    nearest = (nearest + jnp.sum(latent * latent, axis=0, keepdims=True)) * (1.0 / EMB)
    msg[0:EMB, :] = latent
    msg[EMB : EMB + 8, :] = jnp.broadcast_to(nearest, (8, 128))
    tell_peer = remote(msg, msg_peer, msend.at[0], mrecv.at[0], peer)
    tell_next = [
        remote(msg, msg_left, msend.at[1 + core], mrecv.at[1], {"seq": right, "ch": core}) for core in (0, 1)
    ]
    tell_peer.start()

    @pl.when(c == 1)
    def _():
        for copy in tell_next:
            copy.start()

    tell_peer.wait_recv()
    tell_next[0].wait_recv()
    lane = iota((EMB + 8, 128), 1)
    own = jnp.where(c == 0, msg[...], msg_peer[...])
    late = jnp.where(c == 0, msg_peer[...], msg[...])
    whole = jnp.where(lane < 32, msg_left[...], jnp.where(lane < 96, own, late))
    lat_ref[...] = whole[0:EMB, :]
    near_ref[...] = whole[EMB : EMB + 8, :]

    tell_peer.wait_send()
    for copy in sends:
        copy.wait_send()
    for i in (0, 1):
        mine, theirs = own_tile(i, jnp.where(c == 0, 1280 - 256 * i, 1536 + 256 * i))
        mine.wait()
        theirs.wait()
        next_tile(2 + i)[0].wait_recv()

    @pl.when(c == 0)
    def _():
        for i in (2, 3):
            mine, theirs = own_tile(i, 1280 - 256 * i)
            mine.wait()
            theirs.wait_send()

    @pl.when(c == 1)
    def _():
        for copy in tell_next:
            copy.wait_send()
        for i in (2, 3):
            own_tile(i, 1280 - 256 * i)[1].wait_recv()
            for copy in next_tile(i):
                copy.wait_send()


def on_device(samples, sample_counts, spaced, restore, shrinking, projector, dictionary):
    hbm = pl.BlockSpec(memory_space=pltpu.HBM)
    vmem = pl.BlockSpec(memory_space=pltpu.VMEM)
    dma = pltpu.SemaphoreType.DMA
    sharpest, latent, nearest = pl.pallas_call(
        kernel,
        out_shape=(
            jax.ShapeDtypeStruct((H, SHARD), BF),
            jax.ShapeDtypeStruct((EMB, 128), F32),
            jax.ShapeDtypeStruct((8, 128), F32),
        ),
        in_specs=[pl.BlockSpec(memory_space=pltpu.SMEM)] + [hbm] * 6,
        out_specs=(hbm, vmem, vmem),
        scratch_shapes=[
            pltpu.VMEM((CAP // 128, H, 128), BF),
            pltpu.VMEM((5, 3 * H, C), BF),
            pltpu.VMEM((5, C, H), BF),
            pltpu.VMEM((2, C, 4 * C), BF),
            pltpu.VMEM((3 * EMB, C), BF),
            pltpu.VMEM((EMB, BINS), F32),
            pltpu.VMEM((3 * EMB, BINS), BF),
            pltpu.VMEM((3, 4, 8, 128), I32),
            pltpu.VMEM((8, 128), I32),
            pltpu.VMEM((2, T, C), BF),
            pltpu.VMEM((2, T, H), BF),
            pltpu.VMEM((2, T, H), BF),
            pltpu.VMEM((2, EDGE, H), BF),
            pltpu.VMEM((PAD + 4 * T, C), BF),
            pltpu.VMEM((T, C), BF),
            pltpu.VMEM((HEAD + T + 8, 3 * H), F32),
            pltpu.VMEM((2, HEAD, 3 * H), F32),
            pltpu.VMEM((T, H), BF),
            pltpu.VMEM((8, 4 * T, 128), F32),
            pltpu.VMEM((T, 4 * C), BF),
            pltpu.VMEM((T, C), BF),
            pltpu.VMEM((T2, C), BF),
            pltpu.VMEM((4, C, 256), BF),
            pltpu.VMEM((EMB + 8, 128), F32),
            pltpu.VMEM((EMB + 8, 128), F32),
            pltpu.VMEM((EMB + 8, 128), F32),
            dma((31,)),
            dma((CAP // 128,)),
            dma((29,)),
            dma((29,)),
            dma((3, 3)),
            dma((3, 4)),
            dma((2, 2)),
            dma((2, 2)),
            dma((2,)),
            dma((2,)),
            dma((4,)),
            dma((4, 2)),
            dma((4,)),
            dma((2,)),
            dma((3,)),
            dma((2,)),
        ],
        compiler_params=pltpu.CompilerParams(
            collective_id=0, has_side_effects=True, vmem_limit_bytes=63 * 2**20
        ),
        name="encoder",
    )(sample_counts, samples, spaced, restore, shrinking, projector, dictionary)
    return sharpest, latent, nearest[0]


def solution(mesh):
    return jax.shard_map(
        on_device,
        mesh=mesh,
        in_specs=(
            P("ch", "seq"),
            P("seq"),
            P(None, None, "ch", None),
            P(None, None, "ch"),
            P(None, None, "ch", None),
            P(None, "ch"),
            P(),
        ),
        out_specs=(P("ch", "seq"), P(None, "seq"), P("seq")),
        check_vma=False,
    )
```

time: 530 us -> 97.9 us (0.18)
  waiting for transfers between devices: 285 us -> 0 us
  Pallas kernels: 0 us -> 91.4 us
  matrix products: 74.7 us -> 0 us
  local copies, waits for them, and re-layouts: 77.7 us -> 4.98 us
  starting transfers between devices: 30.1 us -> 0 us
  blocking collectives: 26.8 us -> 0 us
  other arithmetic: 17.2 us -> 0 us
  between operations: 15 us -> 1.3 us
    all_gather x6 -> x0, waiting for transfers between devices: 182 us -> none  [the longest x4 151 us: apply_residual(): pieces = lax.all_gather(extended, 'ch', axis=0, tiled=True)]
    pallas_call x0 -> x1, Pallas kernels: none -> 91.4 us  [on_device(): pl.pallas_call(kernel, out_shape=(jax.ShapeDtypeStruct((H, SHARD), BF), j...]
    dot_general x25 -> x0, matrix products: 74.7 us -> none  [the longest x5 29.6 us: apply_residual(): jnp.dot(w_two, hidden, preferred_element_type=jnp.float32)]
    reduce_scatter x5 -> x0, waiting for transfers between devices: 71.7 us -> none  [apply_residual(): lax.psum_scatter(jnp.dot(w_two, hidden, preferred_element_type=jnp.float3...]
    slice x13 -> x0, local copies, waits for them, and re-layouts: 40.3 us -> none  [the longest x8 40.2 us: skipping_contraction(): pieces[:, k::4]]
    ppermute x11 -> x0, waiting for transfers between devices: 31 us -> none  [the longest x1 15.8 us: shifted(): lax.ppermute(value, axis, [(source, source + steps) for source in range(l...]
    ppermute x11 -> x0, starting transfers between devices: 29.3 us -> none  [the longest x5 18 us: padded_2(): lax.ppermute(tail, axis, [(i, (i + 1) % count) for i in range(ends)])]
    concatenate x2 -> x0, local copies, waits for them, and re-layouts: 25.7 us -> none  [padded_2(): jnp.concatenate([lax.ppermute(tail, axis, [(i, (i + 1) % count) for i in...]
  transfers between devices with their start and end apart: 22 -> 0, of which waited for: 18 -> 0; matrix products, arithmetic and copies ran while one was open for 0% -> 0% of each run, Pallas kernels for 0% -> 0%
where the time goes in v1:
time: 97.9 us; the launch traced here: 97.6 us
  Pallas kernels  91.4 us (93%)
  local copies, waits for them, and re-layouts  4.98 us (5%)
  between operations  1.3 us (1%)
    pallas_call x1, Pallas kernels, on_device(): pl.pallas_call(kernel, out_shape=(jax.ShapeDtypeStruct((H, SHARD), BF), j...  91.4 us
    unnamed x4, local copies, waits for them, and re-layouts  3.78 us

profile of v1, /device:TPU:1, one launch (start us, length us, event | category | flops | bytes accessed | tf_op | source)
XLA Modules:
  0.0 97.6 jit_solution(5216098235207253411)
XLA Ops:
  1.3 91.4 %encoder.1 = (bf16[512,2048]{1,0:T(8,128)(2,1)}, f32[64,128]{1,0:T(8,128)}, f32[8,128]{1,0:T(8,128)}) custom-call(s32[1]{0:T(128)S(6)} %copy.12.cnt_ref, bf16[512,3072]{1,0:T(8,128)(2,1)} %res_hbm.1, bf16[5,3,256,1024]{3,2,1,0:T(8,128)(2,1)} %w1_hbm.1, bf16[5,1024,256]{2,1,0:T(8,128)(2,1)} %w2_hbm.1, bf16[2,4,512,1024]{3,2,1,0:T(8,128)(2,1)} %dn_hbm.1, ...), custom_call_target="tpu_custom_call" | custom-call | tf_op jit(solution)/shard_map/encoder/pallas_call | solution.py:454
  92.7 0.0 copy-start
  92.7 1.2 %slice_bitcast_fusion = f32[128]{0:T(128)} fusion(f32[8,128]{1,0:T(8,128)} %get-tuple-element.8), kind=kLoop, calls=%fused_computation | loop fusion | bytes 1024 | tf_op jit(solution)/shard_map/squeeze | solution.py:512
  93.9 3.2 %copy.13 = bf16[512,2048]{1,0:T(8,128)(2,1)} copy(bf16[512,2048]{1,0:T(8,128)(2,1)} %get-tuple-element.12) | data formatting | bytes 4194304
  97.0 0.0 copy-done
  97.0 0.6 copy.14
Async XLA Ops:
  92.7 4.4 %copy-start = (f32[64,128]{1,0:T(8,128)S(1)}, f32[64,128]{1,0:T(8,128)}, u32[]{:S(2)}) copy-start(f32[64,128]{1,0:T(8,128)} %get-tuple-element.13) | copy-start | bytes 98308

commit v2 on v1

--- a/solution.py
+++ b/solution.py
@@ -210,55 +210,43 @@
         sends[-1].start()
 
     def block(ref, at, rows, b, dilation, lag, bound, wide_at):
-        def tap(n, _):
-            lanes = pl.ds(pl.multiple_of(256 * n, 256), 256)
+        for n in range(6):
+            lanes = pl.ds(256 * n, 256)
             pb[HEAD : HEAD + rows, lanes] = nt(a[:rows, :], w1[b, lanes, :])
-            return 0
-
-        lax.fori_loop(0, 6, tap, 0)
-
-        def hide(n, _):
-            here = HEAD - lag
+
+        here = HEAD - lag
+        for n in range(4):
 
             def product(k, start):
-                return pb[start : start + rows, pl.ds(pl.multiple_of(512 * k + 128 * n, 128), 128)]
+                return pb[start : start + rows, pl.ds(512 * k + 128 * n, 128)]
 
             p0, p1, p2 = product(0, here - dilation), product(1, here), product(2, here + dilation)
             if bound is not None:
                 t = iota((rows, 128), 0) - jnp.where(last, bound, 1 << 20)
                 p0 = jnp.where((t >= 0) & (t < dilation), 0.0, p0)
                 p2 = jnp.where((t < 0) & (t >= -dilation), 0.0, p2)
-            hid[:rows, pl.ds(pl.multiple_of(128 * n, 128), 128)] = jnp.maximum(p0 + p1 + p2, 0.0).astype(BF)
-            return 0
-
-        lax.fori_loop(0, 4, hide, 0)
+            hid[:rows, pl.ds(128 * n, 128)] = jnp.maximum(p0 + p1 + p2, 0.0).astype(BF)
         if lag:
             carry[b] = pb[rows : rows + HEAD, :]
 
-        def back(n, _):
-            lanes = pl.ds(pl.multiple_of(256 * n, 256), 256)
+        for n in range(4):
+            lanes = pl.ds(256 * n, 256)
             update = nt(hid[:rows, :], w2[b, lanes, :])
             new = (ref[at : at + rows, lanes].astype(F32) + update).astype(BF)
             ref[at : at + rows, lanes] = new
             if wide_at is not None:
                 for q in (0, 1):
                     y32[2 * n + q, wide_at : wide_at + rows, :] = new[:, 128 * q : 128 * (q + 1)].astype(F32)
-            return 0
-
-        lax.fori_loop(0, 4, back, 0)
 
     def out_tile(i):
         r, q = iota((256, 256), 0), iota((256, 256), 1)
         order = ones_where(jnp.where(c == 0, 255 - r, r) == q)
         same = ones_where(r == q)
 
-        def turn(n, _):
-            lanes = pl.ds(pl.multiple_of(256 * n, 256), 256)
+        for n in range(4):
+            lanes = pl.ds(256 * n, 256)
             rows = nn(order, x[PAD + 96 + 256 * i : PAD + 352 + 256 * i, lanes]).astype(BF)
             ot[i, lanes, :] = nt(same, rows).astype(BF)
-            return 0
-
-        lax.fori_loop(0, 4, turn, 0)
 
     def half(core):
         return pl.ds(pl.multiple_of(512 * core, 512), 512)
@@ -315,15 +303,12 @@
                 ones_where(T * e + iota((T, T), 1) == T * m + iota((T, T), 0) - gap) for e in range(m + 1)
             ]
 
-            def fill(q, _):
-                lanes = pl.ds(pl.multiple_of(256 * q, 256), 256)
+            for q in range(4):
+                lanes = pl.ds(256 * q, 256)
                 total = x[at : at + T, lanes].astype(F32)
                 for e in range(m + 1):
                     total = total + nn(picks[e], edge[e, :, lanes])
                 x[at : at + T, lanes] = total.astype(BF)
-                return 0
-
-            lax.fori_loop(0, 4, fill, 0)
         for b, dilation in ((0, 1), (1, 3)):
             if n == 0:
                 need(block_weights(b))
@@ -352,12 +337,9 @@
     need(down_weights(0))
 
     def down(l, rows, to):
-        def one(n, _):
-            lanes = pl.ds(pl.multiple_of(256 * n, 256), 256)
+        for n in range(4):
+            lanes = pl.ds(256 * n, 256)
             to[:, lanes] = nt(z[:rows, :], dn[l, lanes, :]).astype(BF)
-            return 0
-
-        lax.fori_loop(0, 4, one, 0)
 
     down(0, T, u)
     for b, dilation in ((2, 1), (3, 3)):
@@ -445,6 +427,19 @@
             own_tile(i, 1280 - 256 * i)[1].wait_recv()
             for copy in next_tile(i):
                 copy.wait_send()
+
+
+def hand_over(sharpest, latent, nearest, sharpest_out, latent_out, nearest_out, sem):
+    copies = [
+        pltpu.make_async_copy(sharpest.at[pl.ds(64 * i, 64)], sharpest_out.at[pl.ds(64 * i, 64)], sem.at[i])
+        for i in range(8)
+    ]
+    for copy in copies:
+        copy.start()
+    latent_out[...] = latent[...]
+    nearest_out[...] = nearest[0]
+    for copy in copies:
+        copy.wait()
 
 
 def on_device(samples, sample_counts, spaced, restore, shrinking, projector, dictionary):
@@ -509,7 +504,18 @@
         ),
         name="encoder",
     )(sample_counts, samples, spaced, restore, shrinking, projector, dictionary)
-    return sharpest, latent, nearest[0]
+    return pl.pallas_call(
+        hand_over,
+        out_shape=(
+            jax.ShapeDtypeStruct((H, SHARD), BF),
+            jax.ShapeDtypeStruct((EMB, 128), F32),
+            jax.ShapeDtypeStruct((128,), F32),
+        ),
+        in_specs=[hbm, vmem, vmem],
+        out_specs=(hbm, vmem, vmem),
+        scratch_shapes=[dma((8,))],
+        name="hand_over",
+    )(sharpest, latent, nearest)
 
 
 def solution(mesh):

time: 97.9 us -> 131 us (1.34)
  Pallas kernels: 91.4 us -> 129 us
  local copies, waits for them, and re-layouts: 4.98 us -> 0 us
    pallas_call x0 -> x1, Pallas kernels: none -> 66.1 us  [on_device(): pl.pallas_call(hand_over, out_shape=(jax.ShapeDtypeStruct((H, SHARD), BF)...]
    pallas_call x1, Pallas kernels: 91.4 us -> 62.8 us  [on_device(): pl.pallas_call(kernel, out_shape=(jax.ShapeDtypeStruct((H, SHARD), BF), j...]
    unnamed x4 -> x0, local copies, waits for them, and re-layouts: 3.78 us -> none
where the time goes in v2:
time: 131 us; the launch traced here: 130 us
  Pallas kernels  129 us (98%)
  between operations  1.45 us (1%)
    pallas_call x1, Pallas kernels, on_device(): pl.pallas_call(hand_over, out_shape=(jax.ShapeDtypeStruct((H, SHARD), BF)...  66.1 us
    pallas_call x1, Pallas kernels, on_device(): pl.pallas_call(kernel, out_shape=(jax.ShapeDtypeStruct((H, SHARD), BF), j...  62.8 us

profile of v2, /device:TPU:1, one launch (start us, length us, event | category | flops | bytes accessed | tf_op | source)
XLA Modules:
  0.0 130.3 jit_solution(2977704068968325138)
XLA Ops:
  1.3 62.8 %encoder.1 = (bf16[512,2048]{1,0:T(8,128)(2,1)}, f32[64,128]{1,0:T(8,128)}, f32[8,128]{1,0:T(8,128)}) custom-call(s32[1]{0:T(128)S(6)} %copy.10.cnt_ref, bf16[512,3072]{1,0:T(8,128)(2,1)} %res_hbm.1, bf16[5,3,256,1024]{3,2,1,0:T(8,128)(2,1)} %w1_hbm.1, bf16[5,1024,256]{2,1,0:T(8,128)(2,1)} %w2_hbm.1, bf16[2,4,512,1024]{3,2,1,0:T(8,128)(2,1)} %dn_hbm.1, ...), custom_call_target="tpu_custom_call" | custom-call | tf_op jit(solution)/shard_map/encoder/pallas_call | solution.py:449
  64.1 66.1 %hand_over.1 = (bf16[512,2048]{1,0:T(8,128)(2,1)}, f32[64,128]{1,0:T(8,128)}, f32[128]{0:T(128)}) custom-call(bf16[512,2048]{1,0:T(8,128)(2,1)} %get-tuple-element.6.sharpest, f32[64,128]{1,0:T(8,128)} %get-tuple-element.7.latent, f32[8,128]{1,0:T(8,128)} %get-tuple-element.8.nearest), custom_call_target="tpu_custom_call" | custom-call | tf_op jit(solution)/shard_map/hand_over/pallas_call | solution.py:507

commit v3 on v2

--- a/solution.py
+++ b/solution.py
@@ -429,16 +429,18 @@
                 copy.wait_send()
 
 
-def hand_over(sharpest, latent, nearest, sharpest_out, latent_out, nearest_out, sem):
-    copies = [
-        pltpu.make_async_copy(sharpest.at[pl.ds(64 * i, 64)], sharpest_out.at[pl.ds(64 * i, 64)], sem.at[i])
-        for i in range(8)
-    ]
-    for copy in copies:
+def hand_over(sharpest, latent, nearest, sharpest_out, latent_out, nearest_out, held, sem):
+    parts = [pl.ds(64 * i, 64) for i in range(8)]
+    reads = [pltpu.make_async_copy(sharpest.at[p], held.at[p], sem.at[0, i]) for i, p in enumerate(parts)]
+    writes = [pltpu.make_async_copy(held.at[p], sharpest_out.at[p], sem.at[1, i]) for i, p in enumerate(parts)]
+    for copy in reads:
         copy.start()
     latent_out[...] = latent[...]
     nearest_out[...] = nearest[0]
-    for copy in copies:
+    for read, write in zip(reads, writes):
+        read.wait()
+        write.start()
+    for copy in writes:
         copy.wait()
 
 
@@ -513,7 +515,7 @@
         ),
         in_specs=[hbm, vmem, vmem],
         out_specs=(hbm, vmem, vmem),
-        scratch_shapes=[dma((8,))],
+        scratch_shapes=[pltpu.VMEM((H, SHARD), BF), dma((2, 8))],
         name="hand_over",
     )(sharpest, latent, nearest)
 

time: 131 us -> 68.2 us (0.52)
  Pallas kernels: 129 us -> 66.6 us
    pallas_call x1, Pallas kernels: 66.1 us -> 3.77 us  [on_device(): pl.pallas_call(hand_over, out_shape=(jax.ShapeDtypeStruct((H, SHARD), BF)...]
where the time goes in v3:
time: 68.2 us; the launch traced here: 68 us
  Pallas kernels  66.6 us (98%)
  between operations  1.45 us (2%)
    pallas_call x1, Pallas kernels, on_device(): pl.pallas_call(kernel, out_shape=(jax.ShapeDtypeStruct((H, SHARD), BF), j...  62.8 us
    pallas_call x1, Pallas kernels, on_device(): pl.pallas_call(hand_over, out_shape=(jax.ShapeDtypeStruct((H, SHARD), BF)...  3.77 us

profile of v3, /device:TPU:1, one launch (start us, length us, event | category | flops | bytes accessed | tf_op | source)
XLA Modules:
  0.0 68.0 jit_solution(15399694558165759027)
XLA Ops:
  1.3 62.8 %encoder.1 = (bf16[512,2048]{1,0:T(8,128)(2,1)}, f32[64,128]{1,0:T(8,128)}, f32[8,128]{1,0:T(8,128)}) custom-call(s32[1]{0:T(128)S(6)} %copy.10.cnt_ref, bf16[512,3072]{1,0:T(8,128)(2,1)} %res_hbm.1, bf16[5,3,256,1024]{3,2,1,0:T(8,128)(2,1)} %w1_hbm.1, bf16[5,1024,256]{2,1,0:T(8,128)(2,1)} %w2_hbm.1, bf16[2,4,512,1024]{3,2,1,0:T(8,128)(2,1)} %dn_hbm.1, ...), custom_call_target="tpu_custom_call" | custom-call | tf_op jit(solution)/shard_map/encoder/pallas_call | solution.py:451
  64.1 3.8 %hand_over.1 = (bf16[512,2048]{1,0:T(8,128)(2,1)}, f32[64,128]{1,0:T(8,128)}, f32[128]{0:T(128)}) custom-call(bf16[512,2048]{1,0:T(8,128)(2,1)} %get-tuple-element.6.sharpest, f32[64,128]{1,0:T(8,128)} %get-tuple-element.7.latent, f32[8,128]{1,0:T(8,128)} %get-tuple-element.8.nearest), custom_call_target="tpu_custom_call" | custom-call | tf_op jit(solution)/shard_map/hand_over/pallas_call | solution.py:509

commit v4 on v2

--- a/solution.py
+++ b/solution.py
@@ -10,6 +10,7 @@
 C, H, EMB, BINS, SHARD, CAP = 1024, 512, 64, 2048, 2048, 3072
 T = 304
 T2 = 80
+N_SEQ = 64
 HEAD = 24
 PAD = 32
 EDGE = 2 * T
@@ -34,7 +35,7 @@
 def kernel(
     cnt_ref, res_hbm, w1_hbm, w2_hbm, dn_hbm, pj_hbm, cb_hbm,
     out_hbm, lat_ref, near_ref,
-    res, w1, w2, dn, pj, cb, cbk, counts, place, edge, send_r, send_rr, shift, x, a, pb, carry, hid, y32, z, u, v, ot,
+    res, w1, w2, dn, pj, cb, cbk, counts, place, edge, send_r, send_rr, shift, x, a, pb, carry, hid, y32, z, u, v,
     msg, msg_peer, msg_left,
     lsem, rsem, wsend, wrecv, csend, crecv, esend, erecv, hsend, hrecv, olocal, osend, opeer, oleft, msend, mrecv,
 ):
@@ -43,7 +44,6 @@
     right, left = lax.rem(s + 1, n_seq), lax.rem(s + n_seq - 1, n_seq)
     other = 1 - c
     peer = {"seq": s, "ch": other}
-    rounds = ((lax.rem(s, 4), 1), (lax.rem(s // 4, 4), 4), (s // 16, 16))
     last = (s == n_seq - 1) & (c == 1)
 
     def remote(src, dst, send, recv, where):
@@ -97,14 +97,15 @@
     load_cb.start()
 
     barrier = pltpu.get_barrier_semaphore()
-    greeted = [peer] + [{"seq": chip, "ch": core} for chip in (left, right) for core in (0, 1)]
-    partners = [[], [], []]
-    for dim, (at, stride) in enumerate(rounds):
-        for q in (1, 2, 3):
-            j = lax.rem(at + q, 4)
-            partners[dim].append((j, {"seq": s + (j - at) * stride, "ch": c}))
-            greeted.append(partners[dim][-1][1])
-    for where in greeted:
+    def chip(q):
+        return {"seq": lax.rem(s + q, n_seq), "ch": c}
+
+    def greet(q, _):
+        pl.semaphore_signal(barrier, inc=1, device_id=chip(q), device_id_type=MESH)
+        return 0
+
+    lax.fori_loop(1, N_SEQ, greet, 0)
+    for where in (peer, {"seq": left, "ch": other}, {"seq": right, "ch": other}):
         pl.semaphore_signal(barrier, inc=1, device_id=where, device_id_type=MESH)
 
     cnt = cnt_ref[0]
@@ -120,27 +121,12 @@
         found = jnp.concatenate([res[tile + q] for q in range(4)], axis=1)
         return nt(pick, found).astype(BF)
 
-    def count_round(dim, value):
-        at = rounds[dim][0]
-        counts[dim, at] = value
-        copies = []
-        for q, (j, where) in enumerate(partners[dim]):
-            copies.append(
-                remote(counts.at[dim, at], counts.at[dim, at], csend.at[dim, q], crecv.at[dim, at], where)
-            )
-            copies[-1].start()
-        return copies
-
-    def count_sums(dim):
-        at = rounds[dim][0]
-        for q, (j, where) in enumerate(partners[dim]):
-            remote(counts.at[dim, j], counts.at[dim, j], csend.at[dim, q], crecv.at[dim, j], where).wait_recv()
-        before, total = jnp.zeros((8, 128), I32), jnp.zeros((8, 128), I32)
-        for j in range(4):
-            value = counts[dim, j]
-            total = total + value
-            before = before + jnp.where(j < at, value, 0)
-        return before, total
+    def tell_count(q, _):
+        remote(counts.at[s], counts.at[s], csend.at[0], crecv.at[0], chip(q)).start()
+        return 0
+
+    others = pl.ds(0, N_SEQ - 1)
+    all_counts = remote(counts.at[others], counts.at[others], csend.at[0], crecv.at[0], chip(1))
 
     half_c = pl.ds(pl.multiple_of(512 * c, 512), 512)
     sends = []
@@ -157,27 +143,24 @@
         copy.wait()
     for i in groups[0]:
         weight_local(i).start()
-    pl.semaphore_wait(barrier, len(greeted))
-    sends += count_round(0, jnp.full((8, 128), cnt, I32))
+    pl.semaphore_wait(barrier, N_SEQ + 2)
+    counts[s] = jnp.full((8, 128), cnt, I32)
+    lax.fori_loop(1, N_SEQ, tell_count, 0)
     send_r[0] = picked(cnt - 1, -1)
     send_rr[0] = picked(jnp.int32(0), 1)
     send_edges(0)
-    before, total = count_sums(0)
-    sends += count_round(1, total)
     for i in groups[0]:
         sends.append(weight_remote(i))
         sends[-1].start()
     send_r[1] = picked(cnt - 1 - T, -1)
     send_rr[1] = picked(jnp.int32(T), 1)
     send_edges(1)
-    more, total = count_sums(1)
-    before = before + more
-    sends += count_round(2, total)
     for g in (1, 2):
         for i in groups[g]:
             weight_local(i).start()
-    more, total = count_sums(2)
-    place[...] = before + more - SHARD * s
+    all_counts.wait_recv()
+    earlier = iota((N_SEQ, 8, 128), 0) < s
+    place[...] = jnp.sum(jnp.where(earlier, counts[...], 0), axis=0) - SHARD * s
     offset = place[0, 0]
     gap = jnp.where(c == 0, SHARD // 2 - offset, offset + cnt - SHARD)
 
@@ -190,8 +173,7 @@
         rows = pl.ds(PAD + EDGE * h, EDGE)
         return remote(shift.at[h], x.at[rows, half_c], hsend.at[h], hrecv.at[h], peer)
 
-    for h in (0, 1):
-
+    def place_half(h):
         def shifted(n, _):
             shift[h, pl.ds(pl.multiple_of(T * n, 16), T), :] = window(other, 2 * h + n)
             return 0
@@ -200,11 +182,13 @@
         sends.append(to_peer(h))
         sends[-1].start()
 
-    def placed(n, _):
-        x[pl.ds(pl.multiple_of(PAD + T * n, 16), T), half_c] = window(c, n)
-        return 0
-
-    lax.fori_loop(0, 4, placed, 0)
+        def placed(n, _):
+            x[pl.ds(pl.multiple_of(PAD + EDGE * h + T * n, 16), T), half_c] = window(c, 2 * h + n)
+            return 0
+
+        lax.fori_loop(0, 2, placed, 0)
+
+    place_half(0)
     for i in groups[1]:
         sends.append(weight_remote(i))
         sends[-1].start()
@@ -238,32 +222,21 @@
                 for q in (0, 1):
                     y32[2 * n + q, wide_at : wide_at + rows, :] = new[:, 128 * q : 128 * (q + 1)].astype(F32)
 
-    def out_tile(i):
-        r, q = iota((256, 256), 0), iota((256, 256), 1)
-        order = ones_where(jnp.where(c == 0, 255 - r, r) == q)
-        same = ones_where(r == q)
-
-        for n in range(4):
-            lanes = pl.ds(256 * n, 256)
-            rows = nn(order, x[PAD + 96 + 256 * i : PAD + 352 + 256 * i, lanes]).astype(BF)
-            ot[i, lanes, :] = nt(same, rows).astype(BF)
-
     def half(core):
         return pl.ds(pl.multiple_of(512 * core, 512), 512)
 
-    def own_tile(i, start):
-        columns = pl.ds(pl.multiple_of(start, 256), 256)
+    def own_rows(i, first, count, start):
+        rows, to = pl.ds(PAD + first, count), pl.ds(pl.multiple_of(start, 16), count)
         return (
-            pltpu.make_async_copy(ot.at[i, half(c)], out_hbm.at[:, columns], olocal.at[i]),
-            remote(ot.at[i, half(other)], out_hbm.at[:, columns], osend.at[i, 0], opeer.at[i], peer),
+            lambda: pltpu.make_async_copy(x.at[rows, half(c)], out_hbm.at[to], olocal.at[i]),
+            lambda: remote(x.at[rows, half(other)], out_hbm.at[to], osend.at[i, 0], opeer.at[i], peer),
         )
 
-    def next_tile(i):
-        columns = pl.ds(256 * (i - 2), 256)
+    def next_rows(i, first, count):
         return [
             remote(
-                ot.at[i, pl.ds(512 * core, 512)],
-                out_hbm.at[:, columns],
+                x.at[pl.ds(PAD + first, count), pl.ds(512 * core, 512)],
+                out_hbm.at[pl.ds(first - EDGE, count)],
                 osend.at[i, core],
                 oleft.at[i - 2],
                 {"seq": right, "ch": core},
@@ -271,21 +244,23 @@
             for core in (0, 1)
         ]
 
+    pieces = ((96, 176), (272, 336), (608, 272), (880, 240))
+
     def emit(i):
-        out_tile(i)
+        first, count = pieces[i]
         if i < 2:
-            for copy in own_tile(i, jnp.where(c == 0, 1280 - 256 * i, 1536 + 256 * i)):
-                copy.start()
+            for copy in own_rows(i, first, count, jnp.where(c == 0, 416 + first, 1440 + first)):
+                copy().start()
         else:
 
             @pl.when(c == 0)
             def _():
-                for copy in own_tile(i, 1280 - 256 * i):
-                    copy.start()
+                for copy in own_rows(i, first, count, 416 + first):
+                    copy().start()
 
             @pl.when(c == 1)
             def _():
-                for copy in next_tile(i):
+                for copy in next_rows(i, first, count):
                     copy.start()
 
     for n in range(4):
@@ -309,6 +284,8 @@
                 for e in range(m + 1):
                     total = total + nn(picks[e], edge[e, :, lanes])
                 x[at : at + T, lanes] = total.astype(BF)
+        if n == 1:
+            place_half(1)
         for b, dilation in ((0, 1), (1, 3)):
             if n == 0:
                 need(block_weights(b))
@@ -321,7 +298,7 @@
             for i in groups[2]:
                 sends.append(weight_remote(i))
                 sends[-1].start()
-        for i in ((), (0,), (1, 2), (3,))[n]:
+        for i in ((0,), (), (1, 2), (3,))[n]:
             emit(i)
 
     def fold(rows):
@@ -406,50 +383,65 @@
     tell_peer.wait_send()
     for copy in sends:
         copy.wait_send()
+    all_counts.wait_send()
     for i in (0, 1):
-        mine, theirs = own_tile(i, jnp.where(c == 0, 1280 - 256 * i, 1536 + 256 * i))
-        mine.wait()
-        theirs.wait()
-        next_tile(2 + i)[0].wait_recv()
+        first, count = pieces[i]
+        mine, theirs = own_rows(i, first, count, jnp.where(c == 0, 416 + first, 1440 + first))
+        mine().wait()
+        theirs().wait()
+        next_rows(2 + i, *pieces[2 + i])[0].wait_recv()
 
     @pl.when(c == 0)
     def _():
         for i in (2, 3):
-            mine, theirs = own_tile(i, 1280 - 256 * i)
-            mine.wait()
-            theirs.wait_send()
+            mine, theirs = own_rows(i, *pieces[i], 416 + pieces[i][0])
+            mine().wait()
+            theirs().wait_send()
 
     @pl.when(c == 1)
     def _():
         for copy in tell_next:
             copy.wait_send()
         for i in (2, 3):
-            own_tile(i, 1280 - 256 * i)[1].wait_recv()
-            for copy in next_tile(i):
+            own_rows(i, *pieces[i], 416 + pieces[i][0])[1]().wait_recv()
+            for copy in next_rows(i, *pieces[i]):
                 copy.wait_send()
 
 
-def hand_over(sharpest, latent, nearest, sharpest_out, latent_out, nearest_out, sem):
-    copies = [
-        pltpu.make_async_copy(sharpest.at[pl.ds(64 * i, 64)], sharpest_out.at[pl.ds(64 * i, 64)], sem.at[i])
-        for i in range(8)
-    ]
-    for copy in copies:
-        copy.start()
+def hand_over(frames, latent, nearest, sharpest_out, latent_out, nearest_out, rows, columns, sem):
+    def read(j):
+        return pltpu.make_async_copy(frames.at[pl.ds(256 * j, 256)], rows.at[j], sem.at[0, j])
+
+    def write(j):
+        return pltpu.make_async_copy(columns.at[j], sharpest_out.at[:, pl.ds(256 * j, 256)], sem.at[1, j])
+
+    for j in range(8):
+        read(j).start()
     latent_out[...] = latent[...]
     nearest_out[...] = nearest[0]
-    for copy in copies:
-        copy.wait()
+    r, q = iota((256, 256), 0), iota((256, 256), 1)
+    same, reverse = ones_where(r == q), ones_where(255 - r == q)
+    for j in range(8):
+        read(j).wait()
+        to = 7 - j if 2 <= j < 6 else j
+        for h in (0, 1):
+            part = rows[j, :, 256 * h : 256 * (h + 1)]
+            if to != j:
+                part = nn(reverse, part).astype(BF)
+            columns[to, 256 * h : 256 * (h + 1), :] = nt(same, part).astype(BF)
+        write(to).start()
+    for j in range(8):
+        write(j).wait()
 
 
 def on_device(samples, sample_counts, spaced, restore, shrinking, projector, dictionary):
     hbm = pl.BlockSpec(memory_space=pltpu.HBM)
     vmem = pl.BlockSpec(memory_space=pltpu.VMEM)
     dma = pltpu.SemaphoreType.DMA
-    sharpest, latent, nearest = pl.pallas_call(
+    frames, latent, nearest = pl.pallas_call(
         kernel,
         out_shape=(
-            jax.ShapeDtypeStruct((H, SHARD), BF),
+            jax.ShapeDtypeStruct((SHARD, H), BF),
             jax.ShapeDtypeStruct((EMB, 128), F32),
             jax.ShapeDtypeStruct((8, 128), F32),
         ),
@@ -463,7 +455,7 @@
             pltpu.VMEM((3 * EMB, C), BF),
             pltpu.VMEM((EMB, BINS), F32),
             pltpu.VMEM((3 * EMB, BINS), BF),
-            pltpu.VMEM((3, 4, 8, 128), I32),
+            pltpu.VMEM((N_SEQ, 8, 128), I32),
             pltpu.VMEM((8, 128), I32),
             pltpu.VMEM((2, T, C), BF),
             pltpu.VMEM((2, T, H), BF),
@@ -478,7 +470,6 @@
             pltpu.VMEM((T, 4 * C), BF),
             pltpu.VMEM((T, C), BF),
             pltpu.VMEM((T2, C), BF),
-            pltpu.VMEM((4, C, 256), BF),
             pltpu.VMEM((EMB + 8, 128), F32),
             pltpu.VMEM((EMB + 8, 128), F32),
             pltpu.VMEM((EMB + 8, 128), F32),
@@ -486,8 +477,8 @@
             dma((CAP // 128,)),
             dma((29,)),
             dma((29,)),
-            dma((3, 3)),
-            dma((3, 4)),
+            dma((1,)),
+            dma((1,)),
             dma((2, 2)),
             dma((2, 2)),
             dma((2,)),
@@ -513,9 +504,9 @@
         ),
         in_specs=[hbm, vmem, vmem],
         out_specs=(hbm, vmem, vmem),
-        scratch_shapes=[dma((8,))],
+        scratch_shapes=[pltpu.VMEM((8, 256, H), BF), pltpu.VMEM((8, H, 256), BF), dma((2, 8))],
         name="hand_over",
-    )(sharpest, latent, nearest)
+    )(frames, latent, nearest)
 
 
 def solution(mesh):

time: 131 us -> 70.2 us (0.54)
  the two profiles are of different devices: /device:TPU:1 before, /device:TPU:15 now
where the time goes in v4:
time: 70.2 us; the launch traced here: 70 us
  Pallas kernels  68.5 us (98%)
  between operations  1.47 us (2%)
    pallas_call x1, Pallas kernels, on_device(): pl.pallas_call(kernel, out_shape=(jax.ShapeDtypeStruct((SHARD, H), BF), j...  62.4 us
    pallas_call x1, Pallas kernels, on_device(): pl.pallas_call(hand_over, out_shape=(jax.ShapeDtypeStruct((H, SHARD), BF)...  6.12 us

profile of v4, /device:TPU:15, one launch (start us, length us, event | category | flops | bytes accessed | tf_op | source)
XLA Modules:
  0.0 70.0 jit_solution(9638748132042375271)
XLA Ops:
  1.3 62.4 %encoder.1 = (bf16[2048,512]{1,0:T(8,128)(2,1)}, f32[64,128]{1,0:T(8,128)}, f32[8,128]{1,0:T(8,128)}) custom-call(s32[1]{0:T(128)S(6)} %copy.10.cnt_ref, bf16[512,3072]{1,0:T(8,128)(2,1)} %res_hbm.1, bf16[5,3,256,1024]{3,2,1,0:T(8,128)(2,1)} %w1_hbm.1, bf16[5,1024,256]{2,1,0:T(8,128)(2,1)} %w2_hbm.1, bf16[2,4,512,1024]{3,2,1,0:T(8,128)(2,1)} %dn_hbm.1, ...), custom_call_target="tpu_custom_call" | custom-call | tf_op jit(solution)/shard_map/encoder/pallas_call | solution.py:441
  63.7 6.1 %hand_over.1 = (bf16[512,2048]{1,0:T(8,128)(2,1)}, f32[64,128]{1,0:T(8,128)}, f32[128]{0:T(128)}) custom-call(bf16[2048,512]{1,0:T(8,128)(2,1)} %get-tuple-element.6.frames, f32[64,128]{1,0:T(8,128)} %get-tuple-element.7.latent, f32[8,128]{1,0:T(8,128)} %get-tuple-element.8.nearest), custom_call_target="tpu_custom_call" | custom-call | tf_op jit(solution)/shard_map/hand_over/pallas_call | solution.py:498

commit v5 on v4

--- a/solution.py
+++ b/solution.py
@@ -35,7 +35,7 @@
 def kernel(
     cnt_ref, res_hbm, w1_hbm, w2_hbm, dn_hbm, pj_hbm, cb_hbm,
     out_hbm, lat_ref, near_ref,
-    res, w1, w2, dn, pj, cb, cbk, counts, place, edge, send_r, send_rr, shift, x, a, pb, carry, hid, y32, z, u, v,
+    res, w1, w2, dn, pj, cb, cbk, counts, place, edge, send_r, send_rr, shift, x, a, pb, hid, y32, z, u, v,
     msg, msg_peer, msg_left,
     lsem, rsem, wsend, wrecv, csend, crecv, esend, erecv, hsend, hrecv, olocal, osend, opeer, oleft, msend, mrecv,
 ):
@@ -111,7 +111,6 @@
     cnt = cnt_ref[0]
     x[0:PAD, :] = jnp.zeros((PAD, C), BF)
     pb[...] = jnp.zeros(pb.shape, F32)
-    carry[...] = jnp.zeros(carry.shape, F32)
 
     def picked(first, sign):
         lowest = jnp.maximum(jnp.minimum(first, first + sign * (T - 1)), 0)
@@ -193,34 +192,70 @@
         sends.append(weight_remote(i))
         sends[-1].start()
 
-    def block(ref, at, rows, b, dilation, lag, bound, wide_at):
-        for n in range(6):
-            lanes = pl.ds(256 * n, 256)
-            pb[HEAD : HEAD + rows, lanes] = nt(a[:rows, :], w1[b, lanes, :])
-
+    def block(ref, at, rows, b, w, dilation, lag, bound, follow, wide_at):
         here = HEAD - lag
-        for n in range(4):
-
-            def product(k, start):
-                return pb[start : start + rows, pl.ds(512 * k + 128 * n, 128)]
-
-            p0, p1, p2 = product(0, here - dilation), product(1, here), product(2, here + dilation)
-            if bound is not None:
-                t = iota((rows, 128), 0) - jnp.where(last, bound, 1 << 20)
-                p0 = jnp.where((t >= 0) & (t < dilation), 0.0, p0)
-                p2 = jnp.where((t < 0) & (t >= -dilation), 0.0, p2)
-            hid[:rows, pl.ds(128 * n, 128)] = jnp.maximum(p0 + p1 + p2, 0.0).astype(BF)
-        if lag:
-            carry[b] = pb[rows : rows + HEAD, :]
-
-        for n in range(4):
-            lanes = pl.ds(256 * n, 256)
-            update = nt(hid[:rows, :], w2[b, lanes, :])
-            new = (ref[at : at + rows, lanes].astype(F32) + update).astype(BF)
-            ref[at : at + rows, lanes] = new
-            if wide_at is not None:
-                for q in (0, 1):
-                    y32[2 * n + q, wide_at : wide_at + rows, :] = new[:, 128 * q : 128 * (q + 1)].astype(F32)
+
+        def tap(j, k):
+            def step():
+                lanes = pl.ds(512 * k + 256 * j, 256)
+                pb[w, HEAD : HEAD + rows, lanes] = nt(a[w, :rows, :], w1[b, lanes, :])
+
+            return step
+
+        def hide(n):
+            def step():
+                def product(k, start):
+                    return pb[w, start : start + rows, pl.ds(512 * k + 128 * n, 128)]
+
+                p0, p1, p2 = product(0, here - dilation), product(1, here), product(2, here + dilation)
+                if bound is not None:
+                    t = iota((rows, 128), 0) - jnp.where(last, bound, 1 << 20)
+                    p0 = jnp.where((t >= 0) & (t < dilation), 0.0, p0)
+                    p2 = jnp.where((t < 0) & (t >= -dilation), 0.0, p2)
+                hid[w, :rows, pl.ds(128 * n, 128)] = jnp.maximum(p0 + p1 + p2, 0.0).astype(BF)
+
+            return step
+
+        def keep():
+            if lag:
+                pb[w, 0:HEAD, :] = pb[w, rows : rows + HEAD, :]
+
+        def back(n):
+            def step():
+                lanes = pl.ds(256 * n, 256)
+                update = nt(hid[w, :rows, :], w2[b, lanes, :])
+                new = (ref[at : at + rows, lanes].astype(F32) + update).astype(BF)
+                ref[at : at + rows, lanes] = new
+                if follow is not None:
+                    a[follow, :rows, lanes] = jnp.maximum(new, jnp.zeros((), BF))
+                if wide_at is not None:
+                    for q in (0, 1):
+                        y32[2 * n + q, wide_at : wide_at + rows, :] = new[:, 128 * q : 128 * (q + 1)].astype(F32)
+
+            return step
+
+        taps = [tap(j, k) for j in range(2) for k in range(3)]
+        return taps, [hide(n) for n in range(4)], [keep] + [back(n) for n in range(4)]
+
+    def beside(*lists):
+        longest = max(len(steps) for steps in lists)
+        for i in range(longest):
+            for steps in lists:
+                for step in steps[len(steps) * i // longest : len(steps) * (i + 1) // longest]:
+                    step()
+
+    def alone(steps, filler=()):
+        taps, hides, backs = steps
+        beside(taps[:3], list(filler))
+        beside(taps[3:], hides[:2])
+        beside(hides[2:])
+        beside(backs)
+
+    def pair(first, second):
+        beside(first[0])
+        beside(second[0], first[1])
+        beside(first[2], second[1])
+        beside(second[2])
 
     def half(core):
         return pl.ds(pl.multiple_of(512 * core, 512), 512)
@@ -263,73 +298,82 @@
                 for copy in next_rows(i, first, count):
                     copy.start()
 
-    for n in range(4):
+    def fold(first, rows):
+        def one(n):
+            def step():
+                for k in range(4):
+                    lanes = pl.ds(1024 * k + 128 * n, 128)
+                    z[first : first + rows, lanes] = y32[n, pl.ds(4 * first + k, rows, stride=4), :].astype(BF)
+
+            return step
+
+        return [one(n) for n in range(8)]
+
+    def finest(n, b):
+        start = PAD + T * n - 16 * b
+        bound = EDGE - (T * n - 16 * b - 16) if n == 2 else None
+        return block(x, start - 16, T, b, b, (1, 3)[b], 16, bound, None if b else 1, T * n if b else None)
+
+    def ready(n):
         at = PAD + T * n
         if n % 2 == 0:
             to_peer(n // 2).wait_recv()
-        if n >= 2:
-            m = n - 2
-            for core in (0, 1):
-                remote(
-                    send_r.at[m], edge.at[m, :, pl.ds(512 * core, 512)], esend.at[m, 0], erecv.at[m, core],
-                    {"seq": right, "ch": 0},
-                ).wait_recv()
-            picks = [
-                ones_where(T * e + iota((T, T), 1) == T * m + iota((T, T), 0) - gap) for e in range(m + 1)
-            ]
-
-            for q in range(4):
-                lanes = pl.ds(256 * q, 256)
-                total = x[at : at + T, lanes].astype(F32)
-                for e in range(m + 1):
-                    total = total + nn(picks[e], edge[e, :, lanes])
-                x[at : at + T, lanes] = total.astype(BF)
-        if n == 1:
-            place_half(1)
-        for b, dilation in ((0, 1), (1, 3)):
-            if n == 0:
-                need(block_weights(b))
-            start = at - 16 * b
-            a[...] = jnp.maximum(x[start : start + T, :], jnp.zeros((), BF))
-            pb[0:HEAD, :] = carry[b]
-            bound = EDGE - (T * n - 16 * b - 16) if n == 2 else None
-            block(x, start - 16, T, b, dilation, 16, bound, T * n if b == 1 else None)
-        if n == 0:
-            for i in groups[2]:
-                sends.append(weight_remote(i))
-                sends[-1].start()
-        for i in ((0,), (), (1, 2), (3,))[n]:
+        if n < 2:
+            a[0] = jnp.maximum(x[at : at + T, :], jnp.zeros((), BF))
+            return
+        m = n - 2
+        for core in (0, 1):
+            remote(
+                send_r.at[m], edge.at[m, :, pl.ds(512 * core, 512)], esend.at[m, 0], erecv.at[m, core],
+                {"seq": right, "ch": 0},
+            ).wait_recv()
+        picks = [ones_where(T * e + iota((T, T), 1) == T * m + iota((T, T), 0) - gap) for e in range(m + 1)]
+        for q in range(4):
+            lanes = pl.ds(256 * q, 256)
+            total = x[at : at + T, lanes].astype(F32)
+            for e in range(m + 1):
+                total = total + nn(picks[e], edge[e, :, lanes])
+            full = total.astype(BF)
+            x[at : at + T, lanes] = full
+            a[0, :, lanes] = jnp.maximum(full, jnp.zeros((), BF))
+
+    need(block_weights(0))
+    ready(0)
+    alone(finest(0, 0))
+    for i in groups[2]:
+        sends.append(weight_remote(i))
+        sends[-1].start()
+    need(block_weights(1))
+    place_half(1)
+    for n in range(3):
+        ready(n + 1)
+        pair(finest(n, 1), finest(n + 1, 0))
+        for i in ((0,), (), (1, 2))[n]:
             emit(i)
-
-    def fold(rows):
-        def one(n, _):
-            for k in range(4):
-                lanes = pl.ds(pl.multiple_of(1024 * k + 128 * n, 128), 128)
-                z[:rows, lanes] = y32[n, pl.ds(k, rows, stride=4), :].astype(BF)
-            return 0
-
-        lax.fori_loop(0, 8, one, 0)
-
-    fold(T)
+    alone(finest(3, 1), fold(0, 208))
+    emit(3)
+    beside(fold(208, T - 208))
+
     need(down_weights(0))
 
     def down(l, rows, to):
         for n in range(4):
             lanes = pl.ds(256 * n, 256)
-            to[:, lanes] = nt(z[:rows, :], dn[l, lanes, :]).astype(BF)
+            new = nt(z[:rows, :], dn[l, lanes, :]).astype(BF)
+            to[:, lanes] = new
+            a[0, :rows, lanes] = jnp.maximum(new, jnp.zeros((), BF))
 
     down(0, T, u)
-    for b, dilation in ((2, 1), (3, 3)):
-        need(block_weights(b))
-        a[...] = jnp.maximum(u[...], jnp.zeros((), BF))
-        block(u, 0, T, b, dilation, 0, 160, 0 if b == 3 else None)
-
-    fold(T2)
+    need(block_weights(2))
+    need(block_weights(3))
+    alone(block(u, 0, T, 2, 0, 1, 0, 160, 1, None))
+    alone(block(u, 0, T, 3, 1, 3, 0, 160, None, 0))
+
+    beside(fold(0, T2))
     need(down_weights(1))
+    need(block_weights(4))
     down(1, T2, v)
-    need(block_weights(4))
-    a[:T2, :] = jnp.maximum(v[...], jnp.zeros((), BF))
-    block(v, 0, T2, 4, 3, 0, 40, None)
+    alone(block(v, 0, T2, 4, 0, 3, 0, 40, None, None))
 
     need([28])
     load_cb.wait()
@@ -423,13 +467,19 @@
     same, reverse = ones_where(r == q), ones_where(255 - r == q)
     for j in range(8):
         read(j).wait()
-        to = 7 - j if 2 <= j < 6 else j
+
+    def turned(j, to):
         for h in (0, 1):
             part = rows[j, :, 256 * h : 256 * (h + 1)]
             if to != j:
                 part = nn(reverse, part).astype(BF)
             columns[to, 256 * h : 256 * (h + 1), :] = nt(same, part).astype(BF)
-        write(to).start()
+
+    for group in ((0, 1, 6, 7), (2, 3, 4, 5)):
+        for j in group:
+            turned(j, 7 - j if 2 <= j < 6 else j)
+        for j in group:
+            write(j).start()
     for j in range(8):
         write(j).wait()
 
@@ -462,10 +512,9 @@
             pltpu.VMEM((2, T, H), BF),
             pltpu.VMEM((2, EDGE, H), BF),
             pltpu.VMEM((PAD + 4 * T, C), BF),
-            pltpu.VMEM((T, C), BF),
-            pltpu.VMEM((HEAD + T + 8, 3 * H), F32),
-            pltpu.VMEM((2, HEAD, 3 * H), F32),
-            pltpu.VMEM((T, H), BF),
+            pltpu.VMEM((2, T, C), BF),
+            pltpu.VMEM((2, HEAD + T + 8, 3 * H), F32),
+            pltpu.VMEM((2, T, H), BF),
             pltpu.VMEM((8, 4 * T, 128), F32),
             pltpu.VMEM((T, 4 * C), BF),
             pltpu.VMEM((T, C), BF),

time: 70.2 us -> 69 us (0.983)
  Pallas kernels: 68.5 us -> 67.3 us
    pallas_call x1, Pallas kernels: 6.12 us -> 5.17 us  [on_device(): pl.pallas_call(hand_over, out_shape=(jax.ShapeDtypeStruct((H, SHARD), BF)...]
where the time goes in v5:
time: 69 us; the launch traced here: 68.8 us
  Pallas kernels  67.3 us (98%)
  between operations  1.47 us (2%)
    pallas_call x1, Pallas kernels, on_device(): pl.pallas_call(kernel, out_shape=(jax.ShapeDtypeStruct((SHARD, H), BF), j...  62.2 us
    pallas_call x1, Pallas kernels, on_device(): pl.pallas_call(hand_over, out_shape=(jax.ShapeDtypeStruct((H, SHARD), BF)...  5.17 us

profile of v5, /device:TPU:15, one launch (start us, length us, event | category | flops | bytes accessed | tf_op | source)
XLA Modules:
  0.0 68.8 jit_solution(2601737988592260087)
XLA Ops:
  1.3 62.2 %encoder.1 = (bf16[2048,512]{1,0:T(8,128)(2,1)}, f32[64,128]{1,0:T(8,128)}, f32[8,128]{1,0:T(8,128)}) custom-call(s32[1]{0:T(128)S(6)} %copy.10.cnt_ref, bf16[512,3072]{1,0:T(8,128)(2,1)} %res_hbm.1, bf16[5,3,256,1024]{3,2,1,0:T(8,128)(2,1)} %w1_hbm.1, bf16[5,1024,256]{2,1,0:T(8,128)(2,1)} %w2_hbm.1, bf16[2,4,512,1024]{3,2,1,0:T(8,128)(2,1)} %dn_hbm.1, ...), custom_call_target="tpu_custom_call" | custom-call | tf_op jit(solution)/shard_map/encoder/pallas_call | solution.py:491
  63.4 5.2 %hand_over.1 = (bf16[512,2048]{1,0:T(8,128)(2,1)}, f32[64,128]{1,0:T(8,128)}, f32[128]{0:T(128)}) custom-call(bf16[2048,512]{1,0:T(8,128)(2,1)} %get-tuple-element.6.frames, f32[64,128]{1,0:T(8,128)} %get-tuple-element.7.latent, f32[8,128]{1,0:T(8,128)} %get-tuple-element.8.nearest), custom_call_target="tpu_custom_call" | custom-call | tf_op jit(solution)/shard_map/hand_over/pallas_call | solution.py:547

commit v6 on v5

--- a/solution.py
+++ b/solution.py
@@ -14,6 +14,10 @@
 HEAD = 24
 PAD = 32
 EDGE = 2 * T
+
+
+def aligned(at, step):
+    return at if isinstance(at, int) else pl.multiple_of(at, step)
 
 
 def nt(a, b):
@@ -55,16 +59,16 @@
         if i < 15:
             b, k = divmod(i, 3)
             tap = k + (1 - on) * (2 - 2 * k)
-            return w1_hbm.at[b, k], w1.at[b, pl.ds(pl.multiple_of(512 * tap + 256 * c, 256), 256)]
+            return w1_hbm.at[b, k], w1.at[b, pl.ds(aligned(512 * tap + 256 * c, 256), 256)]
         if i < 20:
-            return w2_hbm.at[i - 15], w2.at[i - 15, :, pl.ds(pl.multiple_of(256 * c, 256), 256)]
+            return w2_hbm.at[i - 15], w2.at[i - 15, :, pl.ds(aligned(256 * c, 256), 256)]
         if i < 28:
             l, k = divmod(i - 20, 4)
             tap = k + (1 - on) * (3 - 2 * k)
             return dn_hbm.at[l, k], dn.at[
-                l, pl.ds(pl.multiple_of(512 * c, 512), 512), pl.ds(pl.multiple_of(1024 * tap, 1024), 1024)
+                l, pl.ds(aligned(512 * c, 512), 512), pl.ds(aligned(1024 * tap, 1024), 1024)
             ]
-        return pj_hbm, pj.at[pl.ds(0, EMB), pl.ds(pl.multiple_of(512 * c, 512), 512)]
+        return pj_hbm, pj.at[pl.ds(0, EMB), pl.ds(aligned(512 * c, 512), 512)]
 
     def weight_local(i):
         return pltpu.make_async_copy(*weight(i, c), lsem.at[i])
@@ -114,7 +118,7 @@
 
     def picked(first, sign):
         lowest = jnp.maximum(jnp.minimum(first, first + sign * (T - 1)), 0)
-        tile = jnp.minimum(lax.shift_right_logical(lowest, 7), CAP // 128 - 4)
+        tile = jnp.minimum((lowest >> 7), CAP // 128 - 4)
         column = 128 * tile + iota((T, 512), 1)
         pick = ones_where((column == first + sign * iota((T, 512), 0)) & (column < cnt))
         found = jnp.concatenate([res[tile + q] for q in range(4)], axis=1)
@@ -127,7 +131,7 @@
     others = pl.ds(0, N_SEQ - 1)
     all_counts = remote(counts.at[others], counts.at[others], csend.at[0], crecv.at[0], chip(1))
 
-    half_c = pl.ds(pl.multiple_of(512 * c, 512), 512)
+    half_c = pl.ds(aligned(512 * c, 512), 512)
     sends = []
 
     def send_edges(m):
@@ -146,13 +150,13 @@
     counts[s] = jnp.full((8, 128), cnt, I32)
     lax.fori_loop(1, N_SEQ, tell_count, 0)
     send_r[0] = picked(cnt - 1, -1)
-    send_rr[0] = picked(jnp.int32(0), 1)
+    send_rr[0] = picked(0 * cnt, 1)
     send_edges(0)
     for i in groups[0]:
         sends.append(weight_remote(i))
         sends[-1].start()
     send_r[1] = picked(cnt - 1 - T, -1)
-    send_rr[1] = picked(jnp.int32(T), 1)
+    send_rr[1] = picked(0 * cnt + T, 1)
     send_edges(1)
     for g in (1, 2):
         for i in groups[g]:
@@ -165,7 +169,7 @@
 
     def window(core, n):
         sign = 2 * core - 1
-        first = jnp.where(core == 1, 1440, 1631) + sign * T * n - offset
+        first = 1631 - 191 * core + sign * T * n - offset
         return picked(first, sign)
 
     def to_peer(h):
@@ -174,15 +178,14 @@
 
     def place_half(h):
         def shifted(n, _):
-            shift[h, pl.ds(pl.multiple_of(T * n, 16), T), :] = window(other, 2 * h + n)
+            shift[h, pl.ds(aligned(T * n, 16), T), :] = window(other, 2 * h + n)
             return 0
 
         lax.fori_loop(0, 2, shifted, 0)
-        sends.append(to_peer(h))
-        sends[-1].start()
+        to_peer(h).start()
 
         def placed(n, _):
-            x[pl.ds(pl.multiple_of(PAD + EDGE * h + T * n, 16), T), half_c] = window(c, 2 * h + n)
+            x[pl.ds(aligned(PAD + EDGE * h + T * n, 16), T), half_c] = window(c, 2 * h + n)
             return 0
 
         lax.fori_loop(0, 2, placed, 0)
@@ -192,76 +195,48 @@
         sends.append(weight_remote(i))
         sends[-1].start()
 
-    def block(ref, at, rows, b, w, dilation, lag, bound, follow, wide_at):
-        here = HEAD - lag
-
-        def tap(j, k):
-            def step():
-                lanes = pl.ds(512 * k + 256 * j, 256)
-                pb[w, HEAD : HEAD + rows, lanes] = nt(a[w, :rows, :], w1[b, lanes, :])
-
-            return step
-
-        def hide(n):
-            def step():
-                def product(k, start):
-                    return pb[w, start : start + rows, pl.ds(512 * k + 128 * n, 128)]
-
-                p0, p1, p2 = product(0, here - dilation), product(1, here), product(2, here + dilation)
-                if bound is not None:
-                    t = iota((rows, 128), 0) - jnp.where(last, bound, 1 << 20)
-                    p0 = jnp.where((t >= 0) & (t < dilation), 0.0, p0)
-                    p2 = jnp.where((t < 0) & (t >= -dilation), 0.0, p2)
-                hid[w, :rows, pl.ds(128 * n, 128)] = jnp.maximum(p0 + p1 + p2, 0.0).astype(BF)
-
-            return step
-
-        def keep():
-            if lag:
-                pb[w, 0:HEAD, :] = pb[w, rows : rows + HEAD, :]
-
-        def back(n):
-            def step():
-                lanes = pl.ds(256 * n, 256)
-                update = nt(hid[w, :rows, :], w2[b, lanes, :])
-                new = (ref[at : at + rows, lanes].astype(F32) + update).astype(BF)
-                ref[at : at + rows, lanes] = new
-                if follow is not None:
-                    a[follow, :rows, lanes] = jnp.maximum(new, jnp.zeros((), BF))
-                if wide_at is not None:
-                    for q in (0, 1):
-                        y32[2 * n + q, wide_at : wide_at + rows, :] = new[:, 128 * q : 128 * (q + 1)].astype(F32)
-
-            return step
-
-        taps = [tap(j, k) for j in range(2) for k in range(3)]
-        return taps, [hide(n) for n in range(4)], [keep] + [back(n) for n in range(4)]
-
-    def beside(*lists):
-        longest = max(len(steps) for steps in lists)
-        for i in range(longest):
-            for steps in lists:
-                for step in steps[len(steps) * i // longest : len(steps) * (i + 1) // longest]:
-                    step()
-
-    def alone(steps, filler=()):
-        taps, hides, backs = steps
-        beside(taps[:3], list(filler))
-        beside(taps[3:], hides[:2])
-        beside(hides[2:])
-        beside(backs)
-
-    def pair(first, second):
-        beside(first[0])
-        beside(second[0], first[1])
-        beside(first[2], second[1])
-        beside(second[2])
+    def block(ref, at, rows, b, w, hide, lag, wide_at):
+        for n in range(6):
+            lanes = pl.ds(256 * n, 256)
+            pb[w, HEAD : HEAD + rows, lanes] = nt(a[w, :rows, :], w1[b, lanes, :])
+        hide()
+        if lag:
+            pb[w, 0:HEAD, :] = pb[w, rows : rows + HEAD, :]
+        for n in range(4):
+            lanes = pl.ds(256 * n, 256)
+            update = nt(hid[:rows, :], w2[b, lanes, :])
+            new = (ref[pl.ds(at, rows), lanes].astype(F32) + update).astype(BF)
+            ref[pl.ds(at, rows), lanes] = new
+            a[1 - w, :rows, lanes] = jnp.maximum(new, jnp.zeros((), BF))
+            for q in (0, 1):
+                y32[2 * n + q, pl.ds(wide_at, rows), :] = new[:, 128 * q : 128 * (q + 1)].astype(F32)
+
+    def hidden(first, rows, w, dilation, lag, bound=None):
+        here = HEAD - lag + first
+        for n in range(4):
+
+            def product(k, start):
+                return pb[w, start : start + rows, pl.ds(512 * k + 128 * n, 128)]
+
+            p0, p1, p2 = product(0, here - dilation), product(1, here), product(2, here + dilation)
+            if bound is not None:
+                t = iota((rows, 128), 0) + (first - bound)
+                p0 = jnp.where((t >= 0) & (t < dilation), 0.0, p0)
+                p2 = jnp.where((t < 0) & (t >= -dilation), 0.0, p2)
+            hid[first : first + rows, pl.ds(128 * n, 128)] = jnp.maximum(p0 + p1 + p2, 0.0).astype(BF)
+
+    def hidden_at(rows, w, dilation, lag, bound, here=None):
+        hidden(0, rows, w, dilation, lag)
+
+        @pl.when(last if here is None else last & here)
+        def _():
+            hidden(bound // 16 * 16 - 16, 48, w, dilation, lag, bound)
 
     def half(core):
-        return pl.ds(pl.multiple_of(512 * core, 512), 512)
+        return pl.ds(aligned(512 * core, 512), 512)
 
     def own_rows(i, first, count, start):
-        rows, to = pl.ds(PAD + first, count), pl.ds(pl.multiple_of(start, 16), count)
+        rows, to = pl.ds(PAD + first, count), pl.ds(aligned(start, 16), count)
         return (
             lambda: pltpu.make_async_copy(x.at[rows, half(c)], out_hbm.at[to], olocal.at[i]),
             lambda: remote(x.at[rows, half(other)], out_hbm.at[to], osend.at[i, 0], opeer.at[i], peer),
@@ -284,7 +259,7 @@
     def emit(i):
         first, count = pieces[i]
         if i < 2:
-            for copy in own_rows(i, first, count, jnp.where(c == 0, 416 + first, 1440 + first)):
+            for copy in own_rows(i, first, count, 416 + first + 1024 * c):
                 copy().start()
         else:
 
@@ -298,21 +273,11 @@
                 for copy in next_rows(i, first, count):
                     copy.start()
 
-    def fold(first, rows):
-        def one(n):
-            def step():
-                for k in range(4):
-                    lanes = pl.ds(1024 * k + 128 * n, 128)
-                    z[first : first + rows, lanes] = y32[n, pl.ds(4 * first + k, rows, stride=4), :].astype(BF)
-
-            return step
-
-        return [one(n) for n in range(8)]
-
-    def finest(n, b):
-        start = PAD + T * n - 16 * b
-        bound = EDGE - (T * n - 16 * b - 16) if n == 2 else None
-        return block(x, start - 16, T, b, b, (1, 3)[b], 16, bound, None if b else 1, T * n if b else None)
+    def fold(rows):
+        for n in range(8):
+            for k in range(4):
+                lanes = pl.ds(1024 * k + 128 * n, 128)
+                z[:rows, lanes] = y32[n, pl.ds(k, rows, stride=4), :].astype(BF)
 
     def ready(n):
         at = PAD + T * n
@@ -338,22 +303,43 @@
             a[0, :, lanes] = jnp.maximum(full, jnp.zeros((), BF))
 
     need(block_weights(0))
-    ready(0)
-    alone(finest(0, 0))
-    for i in groups[2]:
-        sends.append(weight_remote(i))
-        sends[-1].start()
     need(block_weights(1))
-    place_half(1)
-    for n in range(3):
-        ready(n + 1)
-        pair(finest(n, 1), finest(n + 1, 0))
-        for i in ((0,), (), (1, 2))[n]:
-            emit(i)
-    alone(finest(3, 1), fold(0, 208))
-    emit(3)
-    beside(fold(208, T - 208))
-
+
+    def finest(i, _):
+        n, b = i >> 1, i & 1
+        for chunk in range(4):
+
+            @pl.when(i == 2 * chunk)
+            def _():
+                if chunk == 1:
+                    place_half(1)
+                    for g in groups[2]:
+                        weight_remote(g).start()
+                ready(chunk)
+
+        def hide():
+            for which in (0, 1):
+
+                @pl.when(b == which)
+                def _():
+                    hidden_at(T, which, (1, 3)[which], 16, 16 + 16 * which, n == 2)
+
+        at = aligned(PAD + T * n - 16 * b - 16, 16)
+        block(x, at, T, b, b, hide, 16, aligned(T * n, 16))
+        for chunk, ones in enumerate(((0,), (), (1, 2), (3,))):
+            if ones:
+
+                @pl.when(i == 2 * chunk + 1)
+                def _():
+                    for one in ones:
+                        emit(one)
+
+        return 0
+
+    lax.fori_loop(0, 8, finest, 0)
+    sends += [weight_remote(g) for g in groups[2]] + [to_peer(0), to_peer(1)]
+
+    fold(T)
     need(down_weights(0))
 
     def down(l, rows, to):
@@ -366,14 +352,25 @@
     down(0, T, u)
     need(block_weights(2))
     need(block_weights(3))
-    alone(block(u, 0, T, 2, 0, 1, 0, 160, 1, None))
-    alone(block(u, 0, T, 3, 1, 3, 0, 160, None, 0))
-
-    beside(fold(0, T2))
+
+    def middle(b, _):
+        def hide():
+            for which in (0, 1):
+
+                @pl.when(b == which)
+                def _():
+                    hidden_at(T, which, (1, 3)[which], 0, 160)
+
+        block(u, 0, T, 2 + b, b, hide, 0, 0)
+        return 0
+
+    lax.fori_loop(0, 2, middle, 0)
+
+    fold(T2)
     need(down_weights(1))
     need(block_weights(4))
     down(1, T2, v)
-    alone(block(v, 0, T2, 4, 0, 3, 0, 40, None, None))
+    block(v, 0, T2, 4, 0, lambda: hidden_at(T2, 0, 3, 0, 40), 0, 0)
 
     need([28])
     load_cb.wait()
@@ -430,7 +427,7 @@
     all_counts.wait_send()
     for i in (0, 1):
         first, count = pieces[i]
-        mine, theirs = own_rows(i, first, count, jnp.where(c == 0, 416 + first, 1440 + first))
+        mine, theirs = own_rows(i, first, count, 416 + first + 1024 * c)
         mine().wait()
         theirs().wait()
         next_rows(2 + i, *pieces[2 + i])[0].wait_recv()
@@ -514,7 +511,7 @@
             pltpu.VMEM((PAD + 4 * T, C), BF),
             pltpu.VMEM((2, T, C), BF),
             pltpu.VMEM((2, HEAD + T + 8, 3 * H), F32),
-            pltpu.VMEM((2, T, H), BF),
+            pltpu.VMEM((T, H), BF),
             pltpu.VMEM((8, 4 * T, 128), F32),
             pltpu.VMEM((T, 4 * C), BF),
             pltpu.VMEM((T, C), BF),

time: 69 us -> 73.7 us (1.068)
  Pallas kernels: 67.3 us -> 72.1 us
    pallas_call x1, Pallas kernels: 62.2 us -> 66.9 us  [on_device(): pl.pallas_call(kernel, out_shape=(jax.ShapeDtypeStruct((SHARD, H), BF), j...]
where the time goes in v6:
time: 73.7 us; the launch traced here: 73.5 us
  Pallas kernels  72.1 us (98%)
  between operations  1.45 us (2%)
    pallas_call x1, Pallas kernels, on_device(): pl.pallas_call(kernel, out_shape=(jax.ShapeDtypeStruct((SHARD, H), BF), j...  66.9 us
    pallas_call x1, Pallas kernels, on_device(): pl.pallas_call(hand_over, out_shape=(jax.ShapeDtypeStruct((H, SHARD), BF)...  5.17 us

profile of v6, /device:TPU:15, one launch (start us, length us, event | category | flops | bytes accessed | tf_op | source)
XLA Modules:
  0.0 73.5 jit_solution(7122369201760031209)
XLA Ops:
  1.3 66.9 %encoder.1 = (bf16[2048,512]{1,0:T(8,128)(2,1)}, f32[64,128]{1,0:T(8,128)}, f32[8,128]{1,0:T(8,128)}) custom-call(s32[1]{0:T(128)S(6)} %copy.10.cnt_ref, bf16[512,3072]{1,0:T(8,128)(2,1)} %res_hbm.1, bf16[5,3,256,1024]{3,2,1,0:T(8,128)(2,1)} %w1_hbm.1, bf16[5,1024,256]{2,1,0:T(8,128)(2,1)} %w2_hbm.1, bf16[2,4,512,1024]{3,2,1,0:T(8,128)(2,1)} %dn_hbm.1, ...), custom_call_target="tpu_custom_call" | custom-call | tf_op jit(solution)/shard_map/encoder/pallas_call | solution.py:488
  68.2 5.2 %hand_over.1 = (bf16[512,2048]{1,0:T(8,128)(2,1)}, f32[64,128]{1,0:T(8,128)}, f32[128]{0:T(128)}) custom-call(bf16[2048,512]{1,0:T(8,128)(2,1)} %get-tuple-element.6.frames, f32[64,128]{1,0:T(8,128)} %get-tuple-element.7.latent, f32[8,128]{1,0:T(8,128)} %get-tuple-element.8.nearest), custom_call_target="tpu_custom_call" | custom-call | tf_op jit(solution)/shard_map/hand_over/pallas_call | solution.py:544

commit v7 on v5

--- a/solution.py
+++ b/solution.py
@@ -92,21 +92,20 @@
         pltpu.make_async_copy(res_hbm.at[:, pl.ds(128 * k, 128)], res.at[k], rsem.at[k]) for k in range(CAP // 128)
     ]
     load_cb = pltpu.make_async_copy(cb_hbm, cb, lsem.at[30])
+    barrier = pltpu.get_barrier_semaphore()
+    def chip(q):
+        return {"seq": lax.rem(s + q, n_seq), "ch": c}
+
+    def greet(q, _):
+        pl.semaphore_signal(barrier, inc=1, device_id=chip(q), device_id_type=MESH)
+        return 0
+
+    lax.fori_loop(1, N_SEQ, greet, 0)
+    for where in (peer, {"seq": left, "ch": other}, {"seq": right, "ch": other}):
+        pl.semaphore_signal(barrier, inc=1, device_id=where, device_id_type=MESH)
     for copy in load_res:
         copy.start()
     load_cb.start()
-
-    barrier = pltpu.get_barrier_semaphore()
-    def chip(q):
-        return {"seq": lax.rem(s + q, n_seq), "ch": c}
-
-    def greet(q, _):
-        pl.semaphore_signal(barrier, inc=1, device_id=chip(q), device_id_type=MESH)
-        return 0
-
-    lax.fori_loop(1, N_SEQ, greet, 0)
-    for where in (peer, {"seq": left, "ch": other}, {"seq": right, "ch": other}):
-        pl.semaphore_signal(barrier, inc=1, device_id=where, device_id_type=MESH)
 
     cnt = cnt_ref[0]
     x[0:PAD, :] = jnp.zeros((PAD, C), BF)
@@ -138,26 +137,24 @@
             copy.start()
             sends.append(copy)
 
+    pl.semaphore_wait(barrier, N_SEQ + 2)
+    counts[s] = jnp.full((8, 128), cnt, I32)
+    lax.fori_loop(1, N_SEQ, tell_count, 0)
     for copy in load_res:
         copy.wait()
     for i in groups[0]:
         weight_local(i).start()
-    pl.semaphore_wait(barrier, N_SEQ + 2)
-    counts[s] = jnp.full((8, 128), cnt, I32)
-    lax.fori_loop(1, N_SEQ, tell_count, 0)
-    send_r[0] = picked(cnt - 1, -1)
-    send_rr[0] = picked(jnp.int32(0), 1)
-    send_edges(0)
-    for i in groups[0]:
         sends.append(weight_remote(i))
         sends[-1].start()
-    send_r[1] = picked(cnt - 1 - T, -1)
-    send_rr[1] = picked(jnp.int32(T), 1)
-    send_edges(1)
+    for m in (0, 1):
+        send_r[m] = picked(cnt - 1 - T * m, -1)
+        send_rr[m] = picked(jnp.int32(T * m), 1)
     for g in (1, 2):
         for i in groups[g]:
             weight_local(i).start()
     all_counts.wait_recv()
+    send_edges(0)
+    send_edges(1)
     earlier = iota((N_SEQ, 8, 128), 0) < s
     place[...] = jnp.sum(jnp.where(earlier, counts[...], 0), axis=0) - SHARD * s
     offset = place[0, 0]

time: 69 us -> 63.6 us (0.922)
  the two profiles are of different devices: /device:TPU:15 before, /device:TPU:1 now
where the time goes in v7:
time: 63.6 us; the launch traced here: 63.4 us
  Pallas kernels  61.9 us (97%)
  between operations  1.47 us (2%)
    pallas_call x1, Pallas kernels, on_device(): pl.pallas_call(kernel, out_shape=(jax.ShapeDtypeStruct((SHARD, H), BF), j...  56.8 us
    pallas_call x1, Pallas kernels, on_device(): pl.pallas_call(hand_over, out_shape=(jax.ShapeDtypeStruct((H, SHARD), BF)...  5.17 us

profile of v7, /device:TPU:1, one launch (start us, length us, event | category | flops | bytes accessed | tf_op | source)
XLA Modules:
  0.0 63.4 jit_solution(11000965514429988268)
XLA Ops:
  1.3 56.8 %encoder.1 = (bf16[2048,512]{1,0:T(8,128)(2,1)}, f32[64,128]{1,0:T(8,128)}, f32[8,128]{1,0:T(8,128)}) custom-call(s32[1]{0:T(128)S(6)} %copy.10.cnt_ref, bf16[512,3072]{1,0:T(8,128)(2,1)} %res_hbm.1, bf16[5,3,256,1024]{3,2,1,0:T(8,128)(2,1)} %w1_hbm.1, bf16[5,1024,256]{2,1,0:T(8,128)(2,1)} %w2_hbm.1, bf16[2,4,512,1024]{3,2,1,0:T(8,128)(2,1)} %dn_hbm.1, ...), custom_call_target="tpu_custom_call" | custom-call | tf_op jit(solution)/shard_map/encoder/pallas_call | solution.py:488
  58.0 5.2 %hand_over.1 = (bf16[512,2048]{1,0:T(8,128)(2,1)}, f32[64,128]{1,0:T(8,128)}, f32[128]{0:T(128)}) custom-call(bf16[2048,512]{1,0:T(8,128)(2,1)} %get-tuple-element.6.frames, f32[64,128]{1,0:T(8,128)} %get-tuple-element.7.latent, f32[8,128]{1,0:T(8,128)} %get-tuple-element.8.nearest), custom_call_target="tpu_custom_call" | custom-call | tf_op jit(solution)/shard_map/hand_over/pallas_call | solution.py:544

commit v8 on v7

--- a/solution.py
+++ b/solution.py
@@ -109,7 +109,9 @@
 
     cnt = cnt_ref[0]
     x[0:PAD, :] = jnp.zeros((PAD, C), BF)
-    pb[...] = jnp.zeros(pb.shape, F32)
+    for w in (0, 1):
+        pb[w, 0:HEAD, :] = jnp.zeros((HEAD, 3 * H), F32)
+        pb[w, HEAD + T :, :] = jnp.zeros((8, 3 * H), F32)
 
     def picked(first, sign):
         lowest = jnp.maximum(jnp.minimum(first, first + sign * (T - 1)), 0)
@@ -456,15 +458,12 @@
     def write(j):
         return pltpu.make_async_copy(columns.at[j], sharpest_out.at[:, pl.ds(256 * j, 256)], sem.at[1, j])
 
-    for j in range(8):
+    for j in (0, 1, 6, 7, 2, 3, 4, 5):
         read(j).start()
     latent_out[...] = latent[...]
     nearest_out[...] = nearest[0]
     r, q = iota((256, 256), 0), iota((256, 256), 1)
     same, reverse = ones_where(r == q), ones_where(255 - r == q)
-    for j in range(8):
-        read(j).wait()
-
     def turned(j, to):
         for h in (0, 1):
             part = rows[j, :, 256 * h : 256 * (h + 1)]
@@ -473,6 +472,8 @@
             columns[to, 256 * h : 256 * (h + 1), :] = nt(same, part).astype(BF)
 
     for group in ((0, 1, 6, 7), (2, 3, 4, 5)):
+        for j in group:
+            read(j).wait()
         for j in group:
             turned(j, 7 - j if 2 <= j < 6 else j)
         for j in group:

time: 63.6 us -> 63.5 us (level)
  no operation moved by 1% of the time
where the time goes in v8:
time: 63.5 us; the launch traced here: 63.3 us
  Pallas kernels  61.8 us (97%)
  between operations  1.47 us (2%)
    pallas_call x1, Pallas kernels, on_device(): pl.pallas_call(kernel, out_shape=(jax.ShapeDtypeStruct((SHARD, H), BF), j...  56.8 us
    pallas_call x1, Pallas kernels, on_device(): pl.pallas_call(hand_over, out_shape=(jax.ShapeDtypeStruct((H, SHARD), BF)...  5.03 us

profile of v8, /device:TPU:1, one launch (start us, length us, event | category | flops | bytes accessed | tf_op | source)
XLA Modules:
  0.0 63.3 jit_solution(7638916158755180580)
XLA Ops:
  1.3 56.8 %encoder.1 = (bf16[2048,512]{1,0:T(8,128)(2,1)}, f32[64,128]{1,0:T(8,128)}, f32[8,128]{1,0:T(8,128)}) custom-call(s32[1]{0:T(128)S(6)} %copy.10.cnt_ref, bf16[512,3072]{1,0:T(8,128)(2,1)} %res_hbm.1, bf16[5,3,256,1024]{3,2,1,0:T(8,128)(2,1)} %w1_hbm.1, bf16[5,1024,256]{2,1,0:T(8,128)(2,1)} %w2_hbm.1, bf16[2,4,512,1024]{3,2,1,0:T(8,128)(2,1)} %dn_hbm.1, ...), custom_call_target="tpu_custom_call" | custom-call | tf_op jit(solution)/shard_map/encoder/pallas_call | solution.py:489
  58.0 5.0 %hand_over.1 = (bf16[512,2048]{1,0:T(8,128)(2,1)}, f32[64,128]{1,0:T(8,128)}, f32[128]{0:T(128)}) custom-call(bf16[2048,512]{1,0:T(8,128)(2,1)} %get-tuple-element.6.frames, f32[64,128]{1,0:T(8,128)} %get-tuple-element.7.latent, f32[8,128]{1,0:T(8,128)} %get-tuple-element.8.nearest), custom_call_target="tpu_custom_call" | custom-call | tf_op jit(solution)/shard_map/hand_over/pallas_call | solution.py:545
